TPU v7x, 128 devices: a whole 4x4x4 slice. The times are simulated.
128 devices in a mesh: dp: 16 (over x, z), ctx: 8 (over y, core).
Axes of the slice: x: 4, y: 4, z: 4, core: 2. Of those that a mesh axis runs over, the one named last changes fastest.
Arguments:
- tokens: bfloat16 [16, 1024, 896], P('dp', 'ctx'), may hold values from -6 to 6
- cotangent: bfloat16 [16, 1024, 896], P('dp', 'ctx'), may hold values from -6 to 6
- span_order: int32 [16], replicated, may hold values from 0 to 15, each once
- gain_one: bfloat16 [2, 896], P(None, ('dp', 'ctx')), may hold values from 0.5 to 1.5
- w_qkv: bfloat16 [2, 896, 1152], P(None, ('dp', 'ctx')), may hold values from -0.1875 to 0.1875
- b_qkv: bfloat16 [2, 1152], P(None, ('dp', 'ctx')), may hold values from -3 to 3
- w_out: bfloat16 [2, 896, 896], P(None, ('dp', 'ctx')), may hold values from -0.75 to 0.75
- gain_two: bfloat16 [2, 896], P(None, ('dp', 'ctx')), may hold values from 0.5 to 1.5
- w_gate: bfloat16 [2, 896, 4864], P(None, 'dp', 'ctx'), may hold values from -0.1875 to 0.1875
- w_up: bfloat16 [2, 896, 4864], P(None, 'dp', 'ctx'), may hold values from -0.1875 to 0.1875
- w_down: bfloat16 [2, 4864, 896], P(None, 'ctx', 'dp'), may hold values from -0.125 to 0.125
Outputs:
- result: bfloat16 [16, 1024, 896], P('dp', 'ctx')
- input_grad: float32 [16, 1024, 896], P('dp', 'ctx')
- grad_gain_one: float32 [2, 896], P(None, ('dp', 'ctx'))
- grad_w_qkv: float32 [2, 896, 1152], P(None, ('dp', 'ctx'))
- grad_b_qkv: float32 [2, 1024], P(None, ('dp', 'ctx'))
- grad_b_value: float32 [2, 128], P(None, ('dp', 'ctx'))
- grad_w_out: float32 [2, 896, 896], P(None, ('dp', 'ctx'))
- grad_gain_two: float32 [2, 896], P(None, ('dp', 'ctx'))
- grad_w_gate: float32 [2, 896, 4864], P(None, 'dp', 'ctx')
- grad_w_up: float32 [2, 896, 4864], P(None, 'dp', 'ctx')
- grad_w_down: float32 [2, 4864, 896], P(None, 'ctx', 'dp')
Inputs may be any that keep to these rules, and one draw needn't show every extreme that they name: Storage block j of every sequence (its tokens j * 64 to j * 64 + 63) holds the positions from span_order[j] * 64 on; span_order is a permutation.
All inputs are finite; a program needn't handle non-finite values.
Results may differ from a plain program's by a relative error of at most 0.04.
Values may be sent and summed in bfloat16 or wider, within the bound.
A program may use at most 192 MiB of HBM per device.

v0:
```python
import functools

import jax
import jax.numpy as jnp
from jax import lax
from jax.sharding import PartitionSpec as P

H = 14
KVH = 2
HD = 64
LAYERS = 2


eps_norm = 1e-06
rope_base = 1000000.0
neg_fill = -1e30


def norm_scale(inputs, gain_vec):
    return (
        inputs * lax.rsqrt(jnp.mean(inputs * inputs, axis=-1, keepdims=True) + eps_norm) * gain_vec
    )


def rotate(inputs, positions):
    half_dim = inputs.shape[-1] // 2
    frequency = rope_base ** (-jnp.arange(half_dim, dtype=jnp.float32) * 2.0 / inputs.shape[-1])
    angles = positions.astype(jnp.float32)[:, None] * frequency[None, :]
    cosine_table = jnp.cos(angles)[:, None, :]
    sine_table = jnp.sin(angles)[:, None, :]
    lower_half = inputs[..., :half_dim]
    upper_half = inputs[..., half_dim:]
    return jnp.concatenate(
        [
            lower_half * cosine_table - upper_half * sine_table,
            upper_half * cosine_table + lower_half * sine_table,
        ],
        axis=-1,
    )


def swiglu(gate_pre, up_pre):
    return jax.nn.silu(gate_pre) * up_pre


def inner_rows(left_side, right_side):
    return lax.dot_general(
        left_side, right_side, (((0,), (0,)), ((), ())), preferred_element_type=jnp.float32
    )


def times_transposed(left_side, right_side):
    return lax.dot_general(
        left_side, right_side, (((1,), (1,)), ((), ())), preferred_element_type=jnp.float32
    )


def masked_scores(queries, keys_all, allowed):
    scores = jnp.einsum(
        "skgd,tkd->kgst", queries, keys_all, preferred_element_type=jnp.float32
    ) * queries.shape[-1] ** (-0.5)
    return jnp.where(allowed[None, None], scores, neg_fill)


def attend(operands, allowed):
    queries, keys_all, values_all = operands
    scores = masked_scores(queries, keys_all, allowed)
    highest = jnp.max(scores, axis=-1, keepdims=True)
    log_total = highest + jnp.log(jnp.sum(jnp.exp(scores - highest), axis=-1, keepdims=True))
    soft_weights = jnp.exp(scores - log_total).astype(jnp.bfloat16)
    output = jnp.einsum(
        "kgst,tkd->skgd", soft_weights, values_all, preferred_element_type=jnp.float32
    )
    return (output, log_total)


def attend_back(operands, allowed):
    queries, keys_all, values_all, log_total, grad_out = operands
    scale = queries.shape[-1] ** (-0.5)
    soft_weights = jnp.exp(masked_scores(queries, keys_all, allowed) - log_total)
    grad_soft = jnp.einsum(
        "skgd,tkd->kgst", grad_out, values_all, preferred_element_type=jnp.float32
    )
    grad_values = jnp.einsum(
        "kgst,skgd->tkd",
        soft_weights.astype(jnp.bfloat16),
        grad_out,
        preferred_element_type=jnp.float32,
    )
    grad_scores = soft_weights * (
        grad_soft - jnp.sum(grad_soft * soft_weights, axis=-1, keepdims=True)
    )
    grad_scores = grad_scores.astype(jnp.bfloat16)
    grad_queries = (
        jnp.einsum("kgst,tkd->skgd", grad_scores, keys_all, preferred_element_type=jnp.float32)
        * scale
    )
    grad_keys = (
        jnp.einsum("kgst,skgd->tkd", grad_scores, queries, preferred_element_type=jnp.float32)
        * scale
    )
    return (grad_queries, grad_keys, grad_values)


def fetch_forward(stacked, layer_index):
    current = [array_part[layer_index] for array_part in stacked]
    attn_part = (
        lax.all_gather(current[0], ("dp", "ctx"), axis=0, tiled=True),
        lax.all_gather(current[1], ("dp", "ctx"), axis=0, tiled=True),
        lax.all_gather(current[2], ("dp", "ctx"), axis=0, tiled=True),
        lax.all_gather(current[3], ("dp", "ctx"), axis=0, tiled=True),
        lax.all_gather(current[4], ("dp", "ctx"), axis=0, tiled=True),
    )
    mlp_part = (
        lax.all_gather(current[5], "dp", axis=0, tiled=True),
        lax.all_gather(current[6], "dp", axis=0, tiled=True),
        lax.all_gather(current[7], "dp", axis=1, tiled=True),
    )
    return tuple(attn_part) + tuple(mlp_part)


def fetch_backward(stacked, layer_index):
    current = [array_part[layer_index] for array_part in stacked]
    attn_part = (
        lax.all_gather(current[0], ("dp", "ctx"), axis=0, tiled=True),
        lax.all_gather(current[1], ("dp", "ctx"), axis=0, tiled=True),
        lax.all_gather(current[2], ("dp", "ctx"), axis=0, tiled=True),
        lax.all_gather(current[3], ("dp", "ctx"), axis=0, tiled=True),
        lax.all_gather(current[4], ("dp", "ctx"), axis=0, tiled=True),
    )
    mlp_part = (
        lax.all_gather(current[5], "dp", axis=0, tiled=True),
        lax.all_gather(current[6], "dp", axis=0, tiled=True),
        lax.all_gather(current[7], "dp", axis=1, tiled=True),
    )
    return tuple(attn_part) + tuple(mlp_part)


def layer_forward(inputs, weights, flat_pos, allowed, sequences):
    (
        gain_first,
        qkv_weight,
        qkv_bias,
        out_weight,
        gain_second,
        gate_weight,
        up_weight,
        down_weight,
    ) = weights
    tokens_here, width = inputs.shape
    kv_width = KVH * HD
    groups = H // KVH
    local_len = tokens_here // sequences
    hidden = norm_scale(inputs, gain_first.astype(jnp.float32)).astype(jnp.bfloat16)
    packed = jnp.dot(hidden, qkv_weight, preferred_element_type=jnp.float32) + qkv_bias.astype(
        jnp.float32
    )
    queries = rotate(packed[:, :width].reshape(tokens_here, H, HD), flat_pos).astype(jnp.bfloat16)
    keys_here = rotate(
        packed[:, width : width + kv_width].reshape(tokens_here, KVH, HD), flat_pos
    ).astype(jnp.bfloat16)
    values_here = packed[:, width + kv_width :].astype(jnp.bfloat16)
    keys_all, values_all = (
        lax.all_gather(
            keys_here.reshape(sequences, local_len, kv_width), "ctx", axis=1, tiled=True
        ),
        lax.all_gather(
            values_here.reshape(sequences, local_len, kv_width), "ctx", axis=1, tiled=True
        ),
    )
    whole_len = keys_all.shape[1]
    keys_all = keys_all.reshape(sequences, whole_len, KVH, HD)
    values_all = values_all.reshape(sequences, whole_len, KVH, HD)
    queries_seq = queries.reshape(sequences, local_len, KVH, groups, HD)
    attended, log_total = lax.map(
        functools.partial(attend, allowed=allowed), (queries_seq, keys_all, values_all)
    )
    attended = attended.reshape(tokens_here, width).astype(jnp.bfloat16)
    after_attn = inputs + jnp.dot(attended, out_weight, preferred_element_type=jnp.float32)
    hidden_two = norm_scale(after_attn, gain_second.astype(jnp.float32)).astype(jnp.bfloat16)
    hidden_rows = lax.all_gather(hidden_two, "ctx", axis=0, tiled=True)
    gate_pre = jnp.dot(hidden_rows, gate_weight, preferred_element_type=jnp.float32)
    up_pre = jnp.dot(hidden_rows, up_weight, preferred_element_type=jnp.float32)
    activated = swiglu(gate_pre, up_pre).astype(jnp.bfloat16)
    partial_out = jnp.dot(activated, down_weight, preferred_element_type=jnp.float32)
    output = after_attn + lax.psum_scatter(
        partial_out.astype(jnp.bfloat16), "ctx", scatter_dimension=0, tiled=True
    ).astype(jnp.float32)
    kept = (
        inputs,
        hidden,
        queries_seq,
        keys_all,
        values_all,
        log_total,
        attended,
        after_attn,
        hidden_rows,
        gate_pre,
        up_pre,
        activated,
    )
    return (output, kept)


def layer_backward(grad_output, kept, weights, flat_pos, allowed, sequences):
    (
        gain_first,
        qkv_weight,
        qkv_bias,
        out_weight,
        gain_second,
        gate_weight,
        up_weight,
        down_weight,
    ) = weights
    (
        inputs,
        hidden,
        queries_seq,
        keys_all,
        values_all,
        log_total,
        attended,
        after_attn,
        hidden_rows,
        gate_pre,
        up_pre,
        activated,
    ) = kept
    tokens_here, width = inputs.shape
    kv_width = KVH * HD
    whole_len = keys_all.shape[1]
    down_in = lax.all_gather(grad_output.astype(jnp.bfloat16), "ctx", axis=0, tiled=True)
    grad_down = inner_rows(activated, down_in)
    grad_act = times_transposed(down_in, down_weight)
    unused_out, swiglu_back = jax.vjp(swiglu, gate_pre, up_pre)
    grad_gate, grad_up = swiglu_back(grad_act)
    grad_gate = grad_gate.astype(jnp.bfloat16)
    grad_up = grad_up.astype(jnp.bfloat16)
    grad_gate_w = inner_rows(hidden_rows, grad_gate)
    grad_up_w = inner_rows(hidden_rows, grad_up)
    partial_hidden = times_transposed(grad_gate, gate_weight) + times_transposed(grad_up, up_weight)
    grad_hidden_two = lax.psum_scatter(
        partial_hidden.astype(jnp.bfloat16), "ctx", scatter_dimension=0, tiled=True
    ).astype(jnp.float32)
    unused_out, norm_back_second = jax.vjp(norm_scale, after_attn, gain_second.astype(jnp.float32))
    grad_mid, grad_gain_second = norm_back_second(grad_hidden_two)
    grad_mid = grad_mid + grad_output
    attn_in = grad_mid.astype(jnp.bfloat16)
    grad_out_w = inner_rows(attended, attn_in)
    grad_attended = (
        times_transposed(attn_in, out_weight).astype(jnp.bfloat16).reshape(queries_seq.shape)
    )
    grad_queries, grad_keys, grad_values = lax.map(
        functools.partial(attend_back, allowed=allowed),
        (queries_seq, keys_all, values_all, log_total, grad_attended),
    )
    grad_keys, grad_values = (
        lax.psum_scatter(
            grad_keys.reshape(sequences, whole_len, kv_width).astype(jnp.bfloat16),
            "ctx",
            scatter_dimension=1,
            tiled=True,
        ).astype(jnp.float32),
        lax.psum_scatter(
            grad_values.reshape(sequences, whole_len, kv_width).astype(jnp.bfloat16),
            "ctx",
            scatter_dimension=1,
            tiled=True,
        ).astype(jnp.float32),
    )
    unused_out, rope_query_back = jax.vjp(
        functools.partial(rotate, positions=flat_pos), jnp.zeros((tokens_here, H, HD), jnp.float32)
    )
    unused_out, rope_key_back = jax.vjp(
        functools.partial(rotate, positions=flat_pos),
        jnp.zeros((tokens_here, KVH, HD), jnp.float32),
    )
    grad_query_flat = rope_query_back(grad_queries.reshape(tokens_here, H, HD))[0].reshape(
        tokens_here, width
    )
    grad_key_flat = rope_key_back(grad_keys.reshape(tokens_here, KVH, HD))[0].reshape(
        tokens_here, kv_width
    )
    grad_packed = jnp.concatenate(
        [grad_query_flat, grad_key_flat, grad_values.reshape(tokens_here, kv_width)], axis=1
    ).astype(jnp.bfloat16)
    grad_qkv_w = inner_rows(hidden, grad_packed)
    grad_qkv_b = jnp.sum(grad_packed.astype(jnp.float32), axis=0)
    grad_qk_bias = grad_qkv_b[: width + kv_width]
    grad_value_bias = grad_qkv_b[width + kv_width :]
    grad_hidden = times_transposed(grad_packed, qkv_weight)
    unused_out, norm_back_first = jax.vjp(norm_scale, inputs, gain_first.astype(jnp.float32))
    grad_input, grad_gain_first = norm_back_first(grad_hidden)
    grad_input = grad_input + grad_mid
    attn_sums = (
        lax.psum_scatter(grad_gain_first, ("dp", "ctx"), scatter_dimension=0, tiled=True),
        lax.psum_scatter(grad_qkv_w, ("dp", "ctx"), scatter_dimension=0, tiled=True),
        lax.psum_scatter(grad_qk_bias, ("dp", "ctx"), scatter_dimension=0, tiled=True),
        lax.psum_scatter(grad_value_bias, ("dp", "ctx"), scatter_dimension=0, tiled=True),
        lax.psum_scatter(grad_out_w, ("dp", "ctx"), scatter_dimension=0, tiled=True),
        lax.psum_scatter(grad_gain_second, ("dp", "ctx"), scatter_dimension=0, tiled=True),
    )
    mlp_sums = (
        lax.psum_scatter(
            grad_gate_w.astype(jnp.bfloat16), "dp", scatter_dimension=0, tiled=True
        ).astype(jnp.float32),
        lax.psum_scatter(
            grad_up_w.astype(jnp.bfloat16), "dp", scatter_dimension=0, tiled=True
        ).astype(jnp.float32),
        lax.psum_scatter(
            grad_down.astype(jnp.bfloat16), "dp", scatter_dimension=1, tiled=True
        ).astype(jnp.float32),
    )
    return (grad_input, tuple(attn_sums) + tuple(mlp_sums))


def shards(
    tokens, cotangent, span_order, gain_one, w_qkv, b_qkv, w_out, gain_two, w_gate, w_up, w_down
):
    sequences, local_len, width = tokens.shape
    span_len = local_len // 2
    ctx_place = lax.axis_index("ctx")
    offsets = jnp.arange(span_len, dtype=jnp.int32)
    local_spans = lax.dynamic_slice_in_dim(span_order, 2 * ctx_place, 2)
    local_pos = (local_spans[:, None] * span_len + offsets[None, :]).reshape(local_len)
    all_pos = (span_order[:, None] * span_len + offsets[None, :]).reshape(-1)
    allowed = all_pos[None, :] <= local_pos[:, None]
    flat_pos = jnp.tile(local_pos, sequences)
    stacked = (gain_one, w_qkv, b_qkv, w_out, gain_two, w_gate, w_up, w_down)
    state = tokens.reshape(sequences * local_len, width).astype(jnp.float32)
    kept_layers = []
    for layer_index in range(LAYERS):
        weights = fetch_forward(stacked, layer_index)
        state, kept = layer_forward(state, weights, flat_pos, allowed, sequences)
        kept_layers.append(kept)
    grad_state = cotangent.reshape(sequences * local_len, width).astype(jnp.float32)
    grad_layers = []
    for layer_index in reversed(range(LAYERS)):
        weights = fetch_backward(stacked, layer_index)
        grad_state, layer_sums = layer_backward(
            grad_state, kept_layers[layer_index], weights, flat_pos, allowed, sequences
        )
        grad_layers.insert(0, layer_sums)
    grad_stacks = [
        jnp.stack([layer_sums[member] for layer_sums in grad_layers]) for member in range(9)
    ]
    output = state.astype(jnp.bfloat16).reshape(sequences, local_len, width)
    input_grad = grad_state.reshape(sequences, local_len, width)
    return (
        output,
        input_grad,
        grad_stacks[0],
        grad_stacks[1],
        grad_stacks[2],
        grad_stacks[3],
        grad_stacks[4],
        grad_stacks[5],
        grad_stacks[6],
        grad_stacks[7],
        grad_stacks[8],
    )


def solution(mesh):
    return jax.shard_map(
        shards,
        mesh=mesh,
        in_specs=(
            P("dp", "ctx", None),
            P("dp", "ctx", None),
            P(),
            P(None, ("dp", "ctx")),
            P(None, ("dp", "ctx"), None),
            P(None, ("dp", "ctx")),
            P(None, ("dp", "ctx"), None),
            P(None, ("dp", "ctx")),
            P(None, "dp", "ctx"),
            P(None, "dp", "ctx"),
            P(None, "ctx", "dp"),
        ),
        out_specs=(
            P("dp", "ctx", None),
            P("dp", "ctx", None),
            P(None, ("dp", "ctx")),
            P(None, ("dp", "ctx"), None),
            P(None, ("dp", "ctx")),
            P(None, ("dp", "ctx")),
            P(None, ("dp", "ctx"), None),
            P(None, ("dp", "ctx")),
            P(None, "dp", "ctx"),
            P(None, "dp", "ctx"),
            P(None, "ctx", "dp"),
        ),
        check_vma=False,
    )
```

profile of v0, /device:TPU:0, one launch (start us, length us, event | category | flops | bytes accessed | tf_op | source)
XLA Modules:
  0.0 1627.6 jit_solution(1623748511222581089)
XLA Ops:
  15.5 69.2 %all-reduce.34 = (bf16[1152]{0:T(1024)(128)(2,1)S(1)}, bf16[896]{0:T(1024)(128)(2,1)S(1)}, bf16[896]{0:T(1024)(128)(2,1)S(1)}, bf16[1152]{0:T(1024)(128)(2,1)S(1...) all-reduce(bf16[1152]{0:T(1024)(128)(2,1)S(1)} %dynamic-update-slic, ...), channel_id=4, replica_groups=mesh['dp'=16,'ctx'=8] {'dp','ctx'}, use_global_device_ids=true, to_apply=%add.9 | all-reduce | flops 5888 | bytes 23552
  88.0 2.9 convolution_add_fusion.1
  91.1 11.6 all_gather.90
  102.9 12.8 all-gather.3
  121.9 26.4 %all-gather.42.cloned.1.call-done = bf16[1,896,896]{2,0,1:T(2,128)(2,1)} async-done(((bf16[1,7,896]{2,0,1:T(2,128)(2,1)}), bf16[1,896,896]{2,0,1:T(2,128)(2,1)}) %all-gather.42.cloned.1.call-update) | async-done | bytes 1605648 | tf_op jit(solution)/shard_map/all_gather | solution.py:111
  148.3 2.5 multiply_reduce_fusion.4
  153.4 38.2 %all-gather.44.cloned.1.call-done = bf16[1,896,608]{2,1,0:T(8,128)(2,1)} async-done(((bf16[1,56,608]{2,1,0:T(8,128)(2,1)}), bf16[1,896,608]{2,1,0:T(8,128)(2,1)}) %all-gather.44.cloned.1.call-update) | async-done | bytes 1089552 | tf_op jit(solution)/shard_map/all_gather | solution.py:115
  191.6 26.2 %all-gather.34.cloned.1.call-done = bf16[1024,896]{1,0:T(8,128)(2,1)} async-done(((bf16[128,896]{1,0:T(8,128)(2,1)}), bf16[1024,896]{1,0:T(8,128)(2,1)}) %all-gather.34.cloned.1.call-update) | async-done | bytes 1835024 | tf_op jit(solution)/shard_map/all_gather | solution.py:181
  217.8 4.7 fusion.74
  222.5 41.2 %all-gather.46.cloned.1.call-done = bf16[1,896,608]{2,1,0:T(8,128)(2,1)} async-done(((bf16[1,56,608]{2,1,0:T(8,128)(2,1)}), bf16[1,896,608]{2,1,0:T(8,128)(2,1)}) %all-gather.46.cloned.1.call-update) | async-done | bytes 1089552 | tf_op jit(solution)/shard_map/all_gather | solution.py:116
  263.7 6.2 multiply_convert_fusion.3
  269.9 38.3 %all-gather.48.cloned.1.call-done = bf16[1,608,896]{1,2,0:T(8,128)(2,1)} async-done(((bf16[1,608,56]{1,2,0:T(8,128)(2,1)}), bf16[1,608,896]{1,2,0:T(8,128)(2,1)}) %all-gather.48.cloned.1.call-update) | async-done | bytes 1089552 | tf_op jit(solution)/shard_map/all_gather | solution.py:117
  308.1 4.7 convolution_convert_fusion.1
  315.6 29.7 %reduce-scatter.35.cloned.1.call-done = bf16[128,896]{1,0:T(8,128)(2,1)} async-done(((bf16[1024,896]{1,0:T(8,128)(2,1)}), bf16[128,896]{1,0:T(8,128)(2,1)}) %reduce-scatter.35.cloned.1.call-update) | async-done | bytes 229392 | tf_op jit(solution)/shard_map/reduce_scatter | solution.py:186
  346.5 68.1 %all-gather.50.cloned.1.call-done = bf16[1,896,1152]{2,0,1:T(2,128)(2,1)} async-done(((bf16[1,7,1152]{2,0,1:T(2,128)(2,1)}), bf16[1,896,1152]{2,0,1:T(2,128)(2,1)}) %all-gather.50.cloned.1.call-update) | async-done | bytes 2064400 | tf_op jit(solution)/shard_map/all_gather | solution.py:109
  414.6 2.7 convolution_add_fusion
  418.4 11.5 all_gather.101
  430.0 13.0 all-gather.12
  449.2 32.1 %all-gather.52.cloned.1.call-done = bf16[1,896,896]{2,0,1:T(2,128)(2,1)} async-done(((bf16[1,7,896]{2,0,1:T(2,128)(2,1)}), bf16[1,896,896]{2,0,1:T(2,128)(2,1)}) %all-gather.52.cloned.1.call-update) | async-done | bytes 1605648 | tf_op jit(solution)/shard_map/all_gather | solution.py:111
  481.3 2.5 multiply_reduce_fusion.2
  486.9 36.9 %all-gather.56.cloned.1.call-done = bf16[1,896,608]{2,1,0:T(8,128)(2,1)} async-done(((bf16[1,56,608]{2,1,0:T(8,128)(2,1)}), bf16[1,896,608]{2,1,0:T(8,128)(2,1)}) %all-gather.56.cloned.1.call-update) | async-done | bytes 1089552 | tf_op jit(solution)/shard_map/all_gather | solution.py:116
  523.8 26.3 %all-gather.36.cloned.1.call-done = bf16[1024,896]{1,0:T(8,128)(2,1)} async-done(((bf16[128,896]{1,0:T(8,128)(2,1)}), bf16[1024,896]{1,0:T(8,128)(2,1)}) %all-gather.36.cloned.1.call-update) | async-done | bytes 1835024 | tf_op jit(solution)/shard_map/all_gather | solution.py:181
  550.2 4.7 fusion.60
  554.9 41.2 %all-gather.54.cloned.1.call-done = bf16[1,896,608]{2,1,0:T(8,128)(2,1)} async-done(((bf16[1,56,608]{2,1,0:T(8,128)(2,1)}), bf16[1,896,608]{2,1,0:T(8,128)(2,1)}) %all-gather.54.cloned.1.call-update) | async-done | bytes 1089552 | tf_op jit(solution)/shard_map/all_gather | solution.py:115
  596.1 4.8 fusion.64
  600.9 39.8 %all-gather.58.cloned.1.call-done = bf16[1,608,896]{1,2,0:T(8,128)(2,1)} async-done(((bf16[1,608,56]{1,2,0:T(8,128)(2,1)}), bf16[1,608,896]{1,2,0:T(8,128)(2,1)}) %all-gather.58.cloned.1.call-update) | async-done | bytes 1089552 | tf_op jit(solution)/shard_map/all_gather | solution.py:117
  640.7 25.6 %all-gather.60.cloned.1.call-done = bf16[1,1024,896]{2,1,0:T(8,128)(2,1)} async-done(((bf16[1,128,896]{2,1,0:T(8,128)(2,1)}), bf16[1,1024,896]{2,1,0:T(8,128)(2,1)}) %all-gather.60.cloned.1.call-update) | async-done | bytes 1835024 | tf_op jit(solution)/shard_map/all_gather | solution.py:234
  666.3 6.9 multiply_convert_fusion.1
  675.3 3.1 add_convert_fusion.1
  678.5 4.7 convolution_convert_fusion
  683.4 28.5 %reduce-scatter.39.cloned.1.call-done = bf16[128,896]{1,0:T(8,128)(2,1)} async-done(((bf16[1024,896]{1,0:T(8,128)(2,1)}), bf16[128,896]{1,0:T(8,128)(2,1)}) %reduce-scatter.39.cloned.1.call-update) | async-done | bytes 229392 | tf_op jit(solution)/shard_map/reduce_scatter | solution.py:244
  713.6 32.5 %reduce-scatter.37.cloned.1.call-done = bf16[128,896]{1,0:T(8,128)(2,1)} async-done(((bf16[1024,896]{1,0:T(8,128)(2,1)}), bf16[128,896]{1,0:T(8,128)(2,1)}) %reduce-scatter.37.cloned.1.call-update) | async-done | bytes 229392 | tf_op jit(solution)/shard_map/reduce_scatter | solution.py:186
  748.1 2.5 fusion.54
  750.8 4.5 fusion.3
  762.6 5.0 fusion.48
  768.8 2.8 convolution_multiply_fusion.1
  771.8 20.2 %reduce-scatter.43.cloned.1.call-done = bf16[128,128]{1,0:T(8,128)(2,1)} async-done(((bf16[1024,128]{1,0:T(8,128)(2,1)}), bf16[128,128]{1,0:T(8,128)(2,1)}) %reduce-scatter.43.cloned.1.call-update) | async-done | bytes 32784
  793.0 31.3 %reduce-scatter.45.cloned.1.call-done = bf16[128,128]{1,0:T(8,128)(2,1)} async-done(((bf16[1024,128]{1,0:T(8,128)(2,1)}), bf16[128,128]{1,0:T(8,128)(2,1)}) %reduce-scatter.45.cloned.1.call-update) | async-done | bytes 32784
  825.2 3.6 multiply_reduce_fusion
  830.0 23.4 %all-gather.38.cloned.1.call-done = bf16[1024,896]{1,0:T(8,128)(2,1)} async-done(((bf16[128,896]{1,0:T(8,128)(2,1)}), bf16[1024,896]{1,0:T(8,128)(2,1)}) %all-gather.38.cloned.1.call-update) | async-done | bytes 1835024 | tf_op jit(solution)/shard_map/all_gather | solution.py:234
  853.4 5.7 multiply_convert_fusion
  861.3 3.1 add_convert_fusion
  864.5 33.4 %reduce-scatter.41.cloned.1.call-done = bf16[128,896]{1,0:T(8,128)(2,1)} async-done(((bf16[1024,896]{1,0:T(8,128)(2,1)}), bf16[128,896]{1,0:T(8,128)(2,1)}) %reduce-scatter.41.cloned.1.call-update) | async-done | bytes 229392 | tf_op jit(solution)/shard_map/reduce_scatter | solution.py:244
  900.1 2.5 fusion.51
  902.8 4.5 fusion
  914.6 4.9 fusion.50
  920.9 4.6 fusion.36
  925.6 4.6 convolution_convert_fusion.2
  930.3 4.5 convolution_convert_fusion.3
  934.8 4.5 convolution_convert_fusion.4
  939.4 4.6 convolution_convert_fusion.5
  946.7 2.7 convolution_convert_fusion.6
  949.8 2.8 fusion.135
  956.8 19.7 %reduce-scatter.49.cloned.1.call-done = bf16[128,128]{1,0:T(8,128)(2,1)} async-done(((bf16[1024,128]{1,0:T(8,128)(2,1)}), bf16[128,128]{1,0:T(8,128)(2,1)}) %reduce-scatter.49.cloned.1.call-update) | async-done | bytes 32784
  977.5 2.8 fusion.112
  980.5 72.6 %reduce-scatter.61.cloned.1.call-done = bf16[608,56]{0,1:T(8,128)(2,1)} async-done(((bf16[608,896]{0,1:T(8,128)(2,1)}), bf16[608,56]{0,1:T(8,128)(2,1)}) %reduce-scatter.61.cloned.1.call-update) | async-done | bytes 68112
  1053.1 77.1 %reduce-scatter.59.cloned.1.call-done = bf16[608,56]{0,1:T(8,128)(2,1)} async-done(((bf16[608,896]{0,1:T(8,128)(2,1)}), bf16[608,56]{0,1:T(8,128)(2,1)}) %reduce-scatter.59.cloned.1.call-update) | async-done | bytes 68112
  1131.8 75.2 %reduce-scatter.57.cloned.1.call-done = bf16[56,608]{1,0:T(8,128)(2,1)} async-done(((bf16[896,608]{1,0:T(8,128)(2,1)}), bf16[56,608]{1,0:T(8,128)(2,1)}) %reduce-scatter.57.cloned.1.call-update) | async-done | bytes 68112
  1207.0 77.1 %reduce-scatter.55.cloned.1.call-done = bf16[56,608]{1,0:T(8,128)(2,1)} async-done(((bf16[896,608]{1,0:T(8,128)(2,1)}), bf16[56,608]{1,0:T(8,128)(2,1)}) %reduce-scatter.55.cloned.1.call-update) | async-done | bytes 68112
  1285.7 75.0 %reduce-scatter.53.cloned.1.call-done = bf16[56,608]{1,0:T(8,128)(2,1)} async-done(((bf16[896,608]{1,0:T(8,128)(2,1)}), bf16[56,608]{1,0:T(8,128)(2,1)}) %reduce-scatter.53.cloned.1.call-update) | async-done | bytes 68112
  1360.7 77.3 %reduce-scatter.51.cloned.1.call-done = bf16[56,608]{1,0:T(8,128)(2,1)} async-done(((bf16[896,608]{1,0:T(8,128)(2,1)}), bf16[56,608]{1,0:T(8,128)(2,1)}) %reduce-scatter.51.cloned.1.call-update) | async-done | bytes 68112
  1439.9 3.0 fusion.91
  1442.9 65.4 %all-reduce.32 = (f32[896]{0:T(1024)S(1)}, f32[896]{0:T(1024)S(1)}, f32[1024]{0:T(1024)S(1)}, f32[1024]{0:T(1024)S(1)}, f32[128]{0:T(128)S(1)}, /*index=5*/f32[128]{0:T(128)S(1)}, f32[896]{0:T(1024)S(1)}, f32[896]{0:T(1024)S(1)}) all-reduce(f32[896]{0:T(1024)S(1)} %copy-done.36, ...), channel_id=30, replica_groups=mesh['dp'=16,'ctx'=8] {'dp','ctx'}, use_global_device_ids=true, to_apply=%region_25.26.clone | all-reduce | flops 5888 | bytes 47104
  1514.3 103.2 %all-reduce.37.cloned.1.call-done = (f32[896,1152]{1,0:T(8,128)}, f32[896,1152]{1,0:T(8,128)}, f32[896,896]{1,0:T(8,128)}, f32[896,896]{1,0:T(8,128)}) async-done(((f32[896,1152]{1,0:T(8,128)}, f32[896,1152]{1,0:T(8,128)}, f32[896,896]{1,0:T(8,128)}, f32[896,896]{1,0:T(8,128)}), (f32[896,1152]{1,0:T(8,128)}, f32[896,1152]{1,0:T(8,128)}, f32[896,896]{1,0:T(8,128)}, ...) | async-done | bytes 14680080
  (327 shorter events, 88.3 us)
Async XLA Ops:
  7.2 80.8 %all-gather.40.cloned.1.call-start = ((), (), s32[]{:S(2)}) async-start(), calls=%async_computation.21 | async-start | bytes 4161024 | tf_op jit(solution)/shard_map/all_gather | solution.py:109
  8.8 139.5 %all-gather.42.cloned.1.call-start = ((), (), s32[]{:S(2)}) async-start(), calls=%async_computation.22 | async-start | bytes 3236352 | tf_op jit(solution)/shard_map/all_gather | solution.py:111
  10.3 181.3 %all-gather.44.cloned.1.call-start = ((), (), s32[]{:S(2)}) async-start(), calls=%async_computation.23 | async-start | bytes 1218560 | tf_op jit(solution)/shard_map/all_gather | solution.py:115
  12.0 205.8 %all-gather.34.cloned.1.call-start = ((), (), s32[]{:S(2)}) async-start(), calls=%async_computation.14 | async-start | bytes 2064384 | tf_op jit(solution)/shard_map/all_gather | solution.py:181
  84.8 6.2 copy-start.29
  85.9 5.2 copy-start.37
  87.8 63.0 %copy-start.26 = (f32[896]{0:T(1024)}, f32[896]{0:T(1024)S(1)}, u32[]{:S(2)}) copy-start(f32[896]{0:T(1024)S(1)} %convert_element_type.364) | copy-start | bytes 10756
  102.9 14.2 copy-start.6
  102.9 14.2 copy-start.8
  120.1 28.2 %copy-start.5 = (bf16[1,128,896]{2,1,0:T(8,128)(2,1)S(1)}, bf16[1,128,896]{2,1,0:T(8,128)(2,1)}, u32[]{:S(2)}) copy-start(bf16[1,128,896]{2,1,0:T(8,128)(2,1)} %param.11) | copy-start | bytes 688132
  121.9 100.6 %copy-start.20 = (bf16[2,64,7,128]{3,1,2,0:T(8,128)(2,1)}, bf16[2,64,7,128]{3,1,2,0:T(8,128)(2,1)S(1)}, u32[]{:S(2)}) copy-start(bf16[2,64,7,128]{3,1,2,0:T(8,128)(2,1)S(1)} %convolution_convert_fusion.8) | copy-start | bytes 688132
  121.9 29.8 %copy-start.24 = (bf16[2,56,608]{2,1,0:T(8,128)(2,1)S(1)}, bf16[2,56,608]{2,1,0:T(8,128)(2,1)}, u32[]{:S(2)}) copy-start(bf16[2,56,608]{2,1,0:T(8,128)(2,1)} %param.20) | copy-start | bytes 408580
  121.9 30.5 %copy-start.25 = (bf16[2,608,56]{1,2,0:T(8,128)(2,1)S(1)}, bf16[2,608,56]{1,2,0:T(8,128)(2,1)}, u32[]{:S(2)}) copy-start(bf16[2,608,56]{1,2,0:T(8,128)(2,1)} %param.21) | copy-start | bytes 408580
  150.7 71.8 %copy-start.46 = (f32[128]{0:T(128)}, f32[128]{0:T(128)S(1)}, u32[]{:S(2)}) copy-start(f32[128]{0:T(128)S(1)} %get-tuple-element.219) | copy-start | bytes 1540
  150.8 71.7 %copy-start.34 = (f32[128]{0:T(128)}, f32[128]{0:T(128)S(1)}, u32[]{:S(2)}) copy-start(f32[128]{0:T(128)S(1)} %fusion.120) | copy-start | bytes 1540
  151.6 112.1 %all-gather.46.cloned.1.call-start = ((), (), s32[]{:S(2)}) async-start(), calls=%async_computation.24 | async-start | bytes 1218560 | tf_op jit(solution)/shard_map/all_gather | solution.py:116
  152.4 155.8 %all-gather.48.cloned.1.call-start = ((), (), s32[]{:S(2)}) async-start(), calls=%async_computation.25 | async-start | bytes 1218560 | tf_op jit(solution)/shard_map/all_gather | solution.py:117
  153.1 192.2 %reduce-scatter.35.cloned.1.call-start = ((), (), s32[]{:S(2)}) async-start(), calls=%async_computation.15 | async-start | bytes 2064384 | tf_op jit(solution)/shard_map/reduce_scatter | solution.py:186
  312.9 101.7 %all-gather.50.cloned.1.call-start = ((), (), s32[]{:S(2)}) async-start(), calls=%async_computation.26 | async-start | bytes 4161024 | tf_op jit(solution)/shard_map/all_gather | solution.py:109
  313.6 167.6 %all-gather.52.cloned.1.call-start = ((), (), s32[]{:S(2)}) async-start(), calls=%async_computation.27 | async-start | bytes 3236352 | tf_op jit(solution)/shard_map/all_gather | solution.py:111
  314.4 209.5 %all-gather.56.cloned.1.call-start = ((), (), s32[]{:S(2)}) async-start(), calls=%async_computation.29 | async-start | bytes 1218560 | tf_op jit(solution)/shard_map/all_gather | solution.py:116
  315.0 235.2 %all-gather.36.cloned.1.call-start = ((), (), s32[]{:S(2)}) async-start(), calls=%async_computation.16 | async-start | bytes 2064384 | tf_op jit(solution)/shard_map/all_gather | solution.py:181
  315.0 102.3 %copy-start.31 = (f32[896]{0:T(1024)}, f32[896]{0:T(1024)S(1)}, u32[]{:S(2)}) copy-start(f32[896]{0:T(1024)S(1)} %convert_element_type.365) | copy-start | bytes 10756
  346.4 70.9 %copy-start.44 = (f32[128]{0:T(128)}, f32[128]{0:T(128)S(1)}, u32[]{:S(2)}) copy-start(f32[128]{0:T(128)S(1)} %get-tuple-element.174) | copy-start | bytes 1540
  346.5 70.9 %copy-start.39 = (f32[128]{0:T(128)}, f32[128]{0:T(128)S(1)}, u32[]{:S(2)}) copy-start(f32[128]{0:T(128)S(1)} %fusion.121) | copy-start | bytes 1540
  418.3 26.1 %copy-start.10 = (bf16[128,14,32]{0,2,1:T(8,128)(2,1)}, bf16[128,14,32]{0,2,1:T(8,128)(2,1)S(1)}, u32[]{:S(2)}) copy-start(bf16[128,14,32]{0,2,1:T(8,128)(2,1)S(1)} %get-tuple-element.185) | copy-start | bytes 344068
  418.3 26.1 %copy-start.12 = (bf16[128,14,32]{0,2,1:T(8,128)(2,1)}, bf16[128,14,32]{0,2,1:T(8,128)(2,1)S(1)}, u32[]{:S(2)}) copy-start(bf16[128,14,32]{0,2,1:T(8,128)(2,1)S(1)} %get-tuple-element.186) | copy-start | bytes 344068
  449.1 105.8 %copy-start.18 = (bf16[2,64,7,128]{3,1,2,0:T(8,128)(2,1)}, bf16[2,64,7,128]{3,1,2,0:T(8,128)(2,1)S(1)}, u32[]{:S(2)}) copy-start(bf16[2,64,7,128]{3,1,2,0:T(8,128)(2,1)S(1)} %convolution_convert_fusion.7) | copy-start | bytes 688132
  449.2 34.6 %copy-start.28 = (f32[896]{0:T(1024)S(1)}, f32[896]{0:T(1024)}, u32[]{:S(2)}) copy-start(f32[896]{0:T(1024)} %convert_element_type.367) | copy-start | bytes 10756
  484.6 111.5 %all-gather.54.cloned.1.call-start = ((), (), s32[]{:S(2)}) async-start(), calls=%async_computation.28 | async-start | bytes 1218560 | tf_op jit(solution)/shard_map/all_gather | solution.py:115
  485.1 155.5 %all-gather.58.cloned.1.call-start = ((), (), s32[]{:S(2)}) async-start(), calls=%async_computation.30 | async-start | bytes 1218560 | tf_op jit(solution)/shard_map/all_gather | solution.py:117
  485.9 180.4 %all-gather.60.cloned.1.call-start = ((), (), s32[]{:S(2)}) async-start(), calls=%async_computation.31 | async-start | bytes 2064384 | tf_op jit(solution)/shard_map/all_gather | solution.py:234
  486.5 225.4 %reduce-scatter.39.cloned.1.call-start = ((), (), s32[]{:S(2)}) async-start(), calls=%async_computation.18 | async-start | bytes 2064384 | tf_op jit(solution)/shard_map/reduce_scatter | solution.py:244
  666.3 6.9 copy-start.52
  678.5 67.7 %reduce-scatter.37.cloned.1.call-start = ((), (), s32[]{:S(2)}) async-start(), calls=%async_computation.17 | async-start | bytes 2064384 | tf_op jit(solution)/shard_map/reduce_scatter | solution.py:186
  683.2 63.0 %copy-start.17 = (bf16[1,128,896]{2,1,0:T(8,128)(2,1)S(1)}, bf16[1,128,896]{2,1,0:T(8,128)(2,1)}, u32[]{:S(2)}) copy-start(bf16[1,128,896]{2,1,0:T(8,128)(2,1)} %param.12) | copy-start | bytes 688132
  683.2 108.8 %reduce-scatter.43.cloned.1.call-start = ((), (), s32[]{:S(2)}) async-start(), calls=%async_computation.32 | async-start | bytes 294912
  750.8 5.4 slice-start.3
  762.6 61.6 %reduce-scatter.45.cloned.1.call-start = ((), (), s32[]{:S(2)}) async-start(), calls=%async_computation.33 | async-start | bytes 294912
  768.8 56.4 %copy-start.32 = (f32[896]{0:T(1024)S(1)}, f32[896]{0:T(1024)}, u32[]{:S(2)}) copy-start(f32[896]{0:T(1024)} %copy-done.31) | copy-start | bytes 10756
  768.8 56.4 %copy-start.40 = (f32[128]{0:T(128)S(1)}, f32[128]{0:T(128)}, u32[]{:S(2)}) copy-start(f32[128]{0:T(128)} %copy-done.39) | copy-start | bytes 1540
  771.6 81.8 %all-gather.38.cloned.1.call-start = ((), (), s32[]{:S(2)}) async-start(), calls=%async_computation.19 | async-start | bytes 2064384 | tf_op jit(solution)/shard_map/all_gather | solution.py:234
  771.8 57.0 %copy-start.45 = (f32[128]{0:T(128)S(1)}, f32[128]{0:T(128)}, u32[]{:S(2)}) copy-start(f32[128]{0:T(128)} %copy-done.44) | copy-start | bytes 1540
  829.7 68.2 %reduce-scatter.41.cloned.1.call-start = ((), (), s32[]{:S(2)}) async-start(), calls=%async_computation.20 | async-start | bytes 2064384 | tf_op jit(solution)/shard_map/reduce_scatter | solution.py:244
  853.4 5.8 copy-start.49
  861.3 36.5 %copy-start.27 = (f32[896]{0:T(1024)S(1)}, f32[896]{0:T(1024)}, u32[]{:S(2)}) copy-start(f32[896]{0:T(1024)} %copy-done.26) | copy-start | bytes 10756
  861.3 36.5 %copy-start.35 = (f32[128]{0:T(128)S(1)}, f32[128]{0:T(128)}, u32[]{:S(2)}) copy-start(f32[128]{0:T(128)} %copy-done.34) | copy-start | bytes 1540
  864.4 34.6 %copy-start.47 = (f32[128]{0:T(128)S(1)}, f32[128]{0:T(128)}, u32[]{:S(2)}) copy-start(f32[128]{0:T(128)} %copy-done.46) | copy-start | bytes 1540
  864.4 91.5 %reduce-scatter.47.cloned.1.call-start = ((), (), s32[]{:S(2)}) async-start(), calls=%async_computation.34 | async-start | bytes 294912
  902.8 5.4 slice-start.1
  914.6 61.9 %reduce-scatter.49.cloned.1.call-start = ((), (), s32[]{:S(2)}) async-start(), calls=%async_computation.35 | async-start | bytes 294912
  920.6 132.4 %reduce-scatter.61.cloned.1.call-start = ((), (), s32[]{:S(2)}) async-start(), calls=%async_computation.41 | async-start | bytes 1218560
  925.6 204.6 %reduce-scatter.59.cloned.1.call-start = ((), (), s32[]{:S(2)}) async-start(), calls=%async_computation.40 | async-start | bytes 1218560
  930.2 276.8 %reduce-scatter.57.cloned.1.call-start = ((), (), s32[]{:S(2)}) async-start(), calls=%async_computation.39 | async-start | bytes 1218560
  934.8 349.3 %reduce-scatter.55.cloned.1.call-start = ((), (), s32[]{:S(2)}) async-start(), calls=%async_computation.38 | async-start | bytes 1218560
  939.4 4.7 copy-start.19
  939.4 421.4 %reduce-scatter.53.cloned.1.call-start = ((), (), s32[]{:S(2)}) async-start(), calls=%async_computation.37 | async-start | bytes 1218560
  944.0 494.0 %reduce-scatter.51.cloned.1.call-start = ((), (), s32[]{:S(2)}) async-start(), calls=%async_computation.36 | async-start | bytes 1218560
  949.4 668.0 %all-reduce.37.cloned.1.call-start = ((), (), s32[]{:S(2)}) async-start(), calls=%async_computation.42 | async-start | bytes 29360128
  953.5 23.9 %copy-start.30 = (f32[896]{0:T(1024)S(1)}, f32[896]{0:T(1024)}, u32[]{:S(2)}) copy-start(f32[896]{0:T(1024)} %copy-done.29) | copy-start | bytes 10756
  953.5 23.9 %copy-start.38 = (f32[128]{0:T(128)S(1)}, f32[128]{0:T(128)}, u32[]{:S(2)}) copy-start(f32[128]{0:T(128)} %copy-done.37) | copy-start | bytes 1540
  1438.0 4.9 copy-start.33
  1438.0 4.9 copy-start.36
  1439.7 73.6 %copy-start.43 = (f32[128]{0:T(128)S(1)}, f32[128]{0:T(128)}, u32[]{:S(2)}) copy-start(f32[128]{0:T(128)} %copy-done.42) | copy-start | bytes 1540
  (27 other events, 77.8 us)
Sparse Core Ops, SparseCore 0:
  11.6 69.2 all-gather.39
  84.5 63.7 all-gather.41
  151.1 40.5 all-gather.43
  193.7 24.0 all-gather.33
  220.4 43.2 all-gather.45
  265.7 42.3 all-gather.47
  313.0 32.3 reduce-scatter.34
  348.9 65.6 all-gather.49
  417.7 63.5 all-gather.51
  483.3 40.5 all-gather.55
  526.1 24.0 all-gather.35
  552.8 43.2 all-gather.53
  598.3 42.3 all-gather.57
  642.2 24.0 all-gather.59
  678.6 33.2 reduce-scatter.38
  714.2 31.8 reduce-scatter.36
  762.7 29.2 reduce-scatter.42
  794.9 29.2 reduce-scatter.44
  829.8 23.5 all-gather.37
  864.6 33.2 reduce-scatter.40
  914.7 29.3 reduce-scatter.46
  947.1 29.3 reduce-scatter.48
  979.8 73.2 reduce-scatter.60
  1056.6 73.4 reduce-scatter.58
  1133.4 73.5 reduce-scatter.56
  1210.5 73.5 reduce-scatter.54
  1287.2 73.4 reduce-scatter.52
  1364.4 73.5 reduce-scatter.50
  1443.7 173.6 all-reduce.36
where the time goes:
time: 1640 us; the launch traced here: 1630 us
  waiting for transfers between devices  1220 us (74%)
  blocking collectives  184 us (11%)
  matrix products  141 us (9%)
  local copies, waits for them, and re-layouts  33.6 us (2%)
  other arithmetic  30.5 us (2%)
    unnamed x40, waiting for transfers between devices  633 us
    unnamed x2, blocking collectives  135 us
    all_gather x2, waiting for transfers between devices, fetch_forward(): lax.all_gather(current[5], 'dp', axis=0, tiled=True)  79.4 us
    all_gather x2, waiting for transfers between devices, fetch_forward(): lax.all_gather(current[6], 'dp', axis=0, tiled=True)  78.1 us
    all_gather x2, waiting for transfers between devices, fetch_forward(): lax.all_gather(current[7], 'dp', axis=1, tiled=True)  78.1 us
    all_gather x2, waiting for transfers between devices, fetch_forward(): lax.all_gather(current[1], ('dp', 'ctx'), axis=0, tiled=True)  68.1 us
    reduce_scatter x2, waiting for transfers between devices, layer_forward(): lax.psum_scatter(partial_out.astype(jnp.bfloat16), 'ctx', scatter_dimensi...  62.3 us
    reduce_scatter x2, waiting for transfers between devices, layer_backward(): lax.psum_scatter(partial_hidden.astype(jnp.bfloat16), 'ctx', scatter_dime...  61.9 us
  transfers between devices with their start and end apart: 29, of which 27 were waited for; matrix products, arithmetic and copies ran while one was open for 8% of the time, Pallas kernels for 0%

commit v1 on v0

v1 whole, which is shorter than its diff:
```python
import functools

import jax
import jax.numpy as jnp
import numpy as np
from jax import lax
from jax.experimental import pallas as pl
from jax.experimental.pallas import tpu as pltpu
from jax.sharding import PartitionSpec as P

H = 14
KVH = 2
HD = 64
LAYERS = 2
D = 896
QKV = 1152
FS = 608
MESH = pl.DeviceIdType.MESH
BF = jnp.bfloat16
F32 = jnp.float32

eps_norm = 1e-06
rope_base = 1000000.0
neg_fill = -1e30


def place():
    dp = lax.axis_index("dp")
    ctx = lax.axis_index("ctx")
    return lax.div(dp, 4), lax.rem(dp, 4), lax.div(ctx, 2), lax.rem(ctx, 2)


def up1(v):
    return lax.rem(v + 1, 4)


def up2(v):
    return lax.rem(v + 2, 4)


def down1(v):
    return lax.rem(v + 3, 4)


def device(x, z, y, c):
    return (x * 4 + z, y * 2 + c)


def greet(peers):
    barrier = pltpu.get_barrier_semaphore()
    for peer in peers:
        pl.semaphore_signal(barrier, inc=1, device_id=peer, device_id_type=MESH)
    pl.semaphore_wait(barrier, len(peers))


class Mail:
    def __init__(self, send_sem, recv_sem):
        self.send_sem = send_sem
        self.recv_sem = recv_sem
        self.sent = []

    def send(self, slot, src, dst, target):
        copy = pltpu.make_async_remote_copy(
            src_ref=src,
            dst_ref=dst,
            send_sem=self.send_sem.at[slot],
            recv_sem=self.recv_sem.at[slot],
            device_id=target,
            device_id_type=MESH,
        )
        copy.start()
        self.sent.append(copy)

    def take(self, slot, dst, source):
        pltpu.make_async_remote_copy(
            src_ref=dst,
            dst_ref=dst,
            send_sem=self.send_sem.at[slot],
            recv_sem=self.recv_sem.at[slot],
            device_id=source,
            device_id_type=MESH,
        ).wait_recv()

    def finish(self):
        for copy in self.sent:
            copy.wait_send()


def weights_kernel(m_ref, a_ref, mf, af, send_sem, recv_sem, local_sem):
    x, z, y, c = place()
    ctx = 2 * y + c
    mail = Mail(send_sem, recv_sem)
    xp, xm, zp, zm, yp, ym = up1(x), down1(x), up1(z), down1(z), up1(y), down1(y)
    to_xp, to_xm = device(xp, z, y, c), device(xm, z, y, c)
    to_zp, to_zm = device(x, zp, y, c), device(x, zm, y, c)
    to_yp, to_ym = device(x, z, yp, c), device(x, z, ym, c)
    other = device(x, z, y, 1 - c)
    own_m = pltpu.make_async_copy(m_ref, mf.at[:, x, z], local_sem.at[0])
    own_a = pltpu.make_async_copy(a_ref, af.at[:, x, z, ctx], local_sem.at[1])
    own_a.start()
    own_m.start()
    greet([to_xp, to_xm, to_zp, to_zm, to_yp, to_ym, other])

    lo, hi = pl.ds(0, 3), pl.ds(3, 3)
    mail.send(0, a_ref, af.at[:, x, z, ctx], to_xp)
    mail.send(1, a_ref, af.at[:, x, z, ctx], to_xm)
    mail.send(2, m_ref.at[lo], mf.at[lo, x, z], to_xp)
    mail.send(3, m_ref.at[lo], mf.at[lo, x, z], to_xm)
    mail.send(4, m_ref.at[hi], mf.at[hi, x, z], to_zp)
    mail.send(5, m_ref.at[hi], mf.at[hi, x, z], to_zm)
    mail.take(0, af.at[:, xm, z, ctx], to_xm)
    mail.send(6, af.at[0, xm, z, ctx], af.at[0, xm, z, ctx], to_xp)
    mail.take(1, af.at[:, xp, z, ctx], to_xp)
    mail.send(7, af.at[1, xp, z, ctx], af.at[1, xp, z, ctx], to_xm)
    x2, z2, y2 = up2(x), up2(z), up2(y)
    mail.take(6, af.at[0, x2, z, ctx], to_xm)
    mail.take(7, af.at[1, x2, z, ctx], to_xp)
    own_a.wait()
    mail.send(8, af.at[:, :, z, ctx], af.at[:, :, z, ctx], to_zp)
    mail.send(9, af.at[:, :, z, ctx], af.at[:, :, z, ctx], to_zm)
    mail.take(2, mf.at[lo, xm, z], to_xm)
    mail.send(10, mf.at[pl.ds(0, 2), xm, z], mf.at[pl.ds(0, 2), xm, z], to_xp)
    mail.take(3, mf.at[lo, xp, z], to_xp)
    mail.send(11, mf.at[pl.ds(2, 1), xp, z], mf.at[pl.ds(2, 1), xp, z], to_xm)
    mail.take(4, mf.at[hi, x, zm], to_zm)
    mail.send(12, mf.at[pl.ds(3, 1), x, zm], mf.at[pl.ds(3, 1), x, zm], to_zp)
    mail.take(5, mf.at[hi, x, zp], to_zp)
    mail.send(13, mf.at[pl.ds(4, 2), x, zp], mf.at[pl.ds(4, 2), x, zp], to_zm)
    mail.take(8, af.at[:, :, zm, ctx], to_zm)
    mail.send(14, af.at[0, :, zm, ctx], af.at[0, :, zm, ctx], to_zp)
    mail.take(9, af.at[:, :, zp, ctx], to_zp)
    mail.send(15, af.at[1, :, zp, ctx], af.at[1, :, zp, ctx], to_zm)
    mail.take(10, mf.at[pl.ds(0, 2), x2, z], to_xm)
    mail.take(11, mf.at[pl.ds(2, 1), x2, z], to_xp)
    own_m.wait()
    mail.send(16, mf.at[lo, :, z], mf.at[lo, :, z], to_zp)
    mail.send(17, mf.at[lo, :, z], mf.at[lo, :, z], to_zm)
    mail.take(12, mf.at[pl.ds(3, 1), x, z2], to_zm)
    mail.take(13, mf.at[pl.ds(4, 2), x, z2], to_zp)
    mail.send(18, mf.at[hi, x], mf.at[hi, x], to_xp)
    mail.send(19, mf.at[hi, x], mf.at[hi, x], to_xm)
    mail.take(14, af.at[0, :, z2, ctx], to_zm)
    mail.take(15, af.at[1, :, z2, ctx], to_zp)

    def kept(part, row):
        return af.at[part, :, :, 2 * row + c]

    def theirs(part, row):
        return af.at[part, :, :, 2 * row + (1 - c)]

    both = slice(None)
    mail.send(20, kept(both, y), kept(both, y), to_yp)
    mail.send(21, kept(both, y), kept(both, y), to_ym)
    mail.send(22, kept(both, y), kept(both, y), other)
    mail.take(16, mf.at[lo, :, zm], to_zm)
    mail.send(23, mf.at[pl.ds(0, 1), :, zm], mf.at[pl.ds(0, 1), :, zm], to_zp)
    mail.take(17, mf.at[lo, :, zp], to_zp)
    mail.send(24, mf.at[pl.ds(1, 2), :, zp], mf.at[pl.ds(1, 2), :, zp], to_zm)
    mail.take(18, mf.at[hi, xm], to_xm)
    mail.send(25, mf.at[pl.ds(3, 2), xm], mf.at[pl.ds(3, 2), xm], to_xp)
    mail.take(19, mf.at[hi, xp], to_xp)
    mail.send(26, mf.at[pl.ds(5, 1), xp], mf.at[pl.ds(5, 1), xp], to_xm)
    mail.take(20, kept(both, ym), to_ym)
    mail.send(27, kept(0, ym), kept(0, ym), to_yp)
    mail.send(28, kept(both, ym), kept(both, ym), other)
    mail.take(21, kept(both, yp), to_yp)
    mail.send(29, kept(1, yp), kept(1, yp), to_ym)
    mail.send(30, kept(both, yp), kept(both, yp), other)
    mail.take(27, kept(0, y2), to_ym)
    mail.send(31, kept(0, y2), kept(0, y2), other)
    mail.take(29, kept(1, y2), to_yp)
    mail.send(32, kept(1, y2), kept(1, y2), other)
    mail.take(23, mf.at[pl.ds(0, 1), :, z2], to_zm)
    mail.take(24, mf.at[pl.ds(1, 2), :, z2], to_zp)
    mail.take(25, mf.at[pl.ds(3, 2), x2], to_xm)
    mail.take(26, mf.at[pl.ds(5, 1), x2], to_xp)
    mail.take(22, theirs(both, y), other)
    mail.take(28, theirs(both, ym), other)
    mail.take(30, theirs(both, yp), other)
    mail.take(31, theirs(0, y2), other)
    mail.take(32, theirs(1, y2), other)
    mail.finish()


def gather_weights(m_block, a_block):
    return pl.pallas_call(
        weights_kernel,
        out_shape=(
            jax.ShapeDtypeStruct((6, 4, 4, 56, FS), BF),
            jax.ShapeDtypeStruct((2, 4, 4, 8, 16, 1024), BF),
        ),
        in_specs=[pl.BlockSpec(memory_space=pl.ANY)] * 2,
        out_specs=[pl.BlockSpec(memory_space=pl.ANY)] * 2,
        scratch_shapes=[
            pltpu.SemaphoreType.DMA((33,)),
            pltpu.SemaphoreType.DMA((33,)),
            pltpu.SemaphoreType.DMA((2,)),
        ],
        compiler_params=pltpu.CompilerParams(collective_id=1, has_side_effects=True),
        name="gather_weights",
    )(m_block, a_block)


def ctx_gather_kernel(rows, v_ref, o_ref, send_sem, recv_sem, local_sem):
    x, z, y, c = place()
    mail = Mail(send_sem, recv_sem)
    yp, ym, y2 = up1(y), down1(y), up2(y)
    to_yp, to_ym, other = device(x, z, yp, c), device(x, z, ym, c), device(x, z, y, 1 - c)
    own = pltpu.make_async_copy(v_ref, o_ref.at[y, c], local_sem.at[0])
    own.start()
    greet([to_yp, to_ym, other])
    half = rows // 2
    first, second = pl.ds(0, half), pl.ds(half, half)
    mail.send(0, v_ref, o_ref.at[y, c], to_yp)
    mail.send(1, v_ref, o_ref.at[y, c], to_ym)
    mail.send(2, v_ref, o_ref.at[y, c], other)
    mail.take(0, o_ref.at[ym, c], to_ym)
    mail.send(3, o_ref.at[ym, c, first], o_ref.at[ym, c, first], to_yp)
    mail.send(4, o_ref.at[ym, c], o_ref.at[ym, c], other)
    mail.take(1, o_ref.at[yp, c], to_yp)
    mail.send(5, o_ref.at[yp, c, second], o_ref.at[yp, c, second], to_ym)
    mail.send(6, o_ref.at[yp, c], o_ref.at[yp, c], other)
    mail.take(3, o_ref.at[y2, c, first], to_ym)
    mail.send(7, o_ref.at[y2, c, first], o_ref.at[y2, c, first], other)
    mail.take(5, o_ref.at[y2, c, second], to_yp)
    mail.send(8, o_ref.at[y2, c, second], o_ref.at[y2, c, second], other)
    own.wait()
    mail.take(2, o_ref.at[y, 1 - c], other)
    mail.take(4, o_ref.at[ym, 1 - c], other)
    mail.take(6, o_ref.at[yp, 1 - c], other)
    mail.take(7, o_ref.at[y2, 1 - c, first], other)
    mail.take(8, o_ref.at[y2, 1 - c, second], other)
    mail.finish()


def ctx_gather(value, collective_id):
    rows, columns = value.shape
    gathered = pl.pallas_call(
        functools.partial(ctx_gather_kernel, rows),
        out_shape=jax.ShapeDtypeStruct((4, 2, rows, columns), value.dtype),
        in_specs=[pl.BlockSpec(memory_space=pl.ANY)],
        out_specs=pl.BlockSpec(memory_space=pl.ANY),
        scratch_shapes=[
            pltpu.SemaphoreType.DMA((9,)),
            pltpu.SemaphoreType.DMA((9,)),
            pltpu.SemaphoreType.DMA((1,)),
        ],
        compiler_params=pltpu.CompilerParams(collective_id=collective_id, has_side_effects=True),
        name="ctx_gather_%d" % columns,
    )(value)
    return gathered.reshape(8 * rows, columns)


def ctx_scatter_kernel(rows, p_ref, o_ref, near, own, far_a, far_b, got_a, got_b, send_sem, recv_sem):
    x, z, y, c = place()
    mail = Mail(send_sem, recv_sem)
    yp, ym, y2 = up1(y), down1(y), up2(y)
    to_yp, to_ym, other = device(x, z, yp, c), device(x, z, ym, c), device(x, z, y, 1 - c)
    greet([to_yp, to_ym, other])
    half = rows // 2
    first, second = pl.ds(0, half), pl.ds(half, half)
    order = (y2, yp, ym, y)
    for slot, row in enumerate(order):
        mail.send(slot, p_ref.at[row, 1 - c], near.at[slot], other)
    mail.take(0, near.at[0], other)
    own[0] = (p_ref[y2, c].astype(F32) + near[0].astype(F32)).astype(BF)
    mail.send(4, own.at[0, first], far_a, to_yp)
    mail.send(5, own.at[0, second], far_b, to_ym)
    mail.take(1, near.at[1], other)
    mail.take(2, near.at[2], other)
    mail.take(4, far_a, to_ym)
    own[1, second] = (p_ref[yp, c, second].astype(F32) + near[1, second].astype(F32)).astype(BF)
    own[1, first] = (
        p_ref[yp, c, first].astype(F32) + near[1, first].astype(F32) + far_a[...].astype(F32)
    ).astype(BF)
    mail.send(6, own.at[1], got_a, to_yp)
    mail.take(5, far_b, to_yp)
    own[2, first] = (p_ref[ym, c, first].astype(F32) + near[2, first].astype(F32)).astype(BF)
    own[2, second] = (
        p_ref[ym, c, second].astype(F32) + near[2, second].astype(F32) + far_b[...].astype(F32)
    ).astype(BF)
    mail.send(7, own.at[2], got_b, to_ym)
    mail.take(3, near.at[3], other)
    o_ref[...] = p_ref[y, c].astype(F32) + near[3].astype(F32)
    mail.take(6, got_a, to_ym)
    mail.take(7, got_b, to_yp)
    o_ref[...] += got_a[...].astype(F32) + got_b[...].astype(F32)
    mail.finish()


def ctx_scatter(value, collective_id):
    rows, columns = value.shape[0] // 8, value.shape[1]
    return pl.pallas_call(
        functools.partial(ctx_scatter_kernel, rows),
        out_shape=jax.ShapeDtypeStruct((rows, columns), F32),
        in_specs=[pl.BlockSpec(memory_space=pltpu.VMEM)],
        out_specs=pl.BlockSpec(memory_space=pltpu.VMEM),
        scratch_shapes=[
            pltpu.VMEM((4, rows, columns), BF),
            pltpu.VMEM((3, rows, columns), BF),
            pltpu.VMEM((rows // 2, columns), BF),
            pltpu.VMEM((rows // 2, columns), BF),
            pltpu.VMEM((rows, columns), BF),
            pltpu.VMEM((rows, columns), BF),
            pltpu.SemaphoreType.DMA((8,)),
            pltpu.SemaphoreType.DMA((8,)),
        ],
        compiler_params=pltpu.CompilerParams(
            collective_id=collective_id, has_side_effects=True, vmem_limit_bytes=32 * 1024 * 1024
        ),
        name="ctx_scatter_%d" % columns,
    )(value.reshape(4, 2, rows, columns))


def grads_kernel(m_ref, a_ref, mo, ao, m_got, near, far_a, far_b, got_a, got_b, total, a_got, send_sem, recv_sem):
    x, z, y, c = place()
    ctx = 2 * y + c
    mail = Mail(send_sem, recv_sem)
    yp, ym, y2 = up1(y), down1(y), up2(y)
    to_yp, to_ym, other = device(x, z, yp, c), device(x, z, ym, c), device(x, z, y, 1 - c)
    shifts = [(i, j) for i in range(4) for j in range(4) if (i, j) != (0, 0)]

    def ahead(i, j):
        return lax.rem(x + i, 4), lax.rem(z + j, 4)

    def behind(i, j):
        return lax.rem(x + 4 - i, 4), lax.rem(z + 4 - j, 4)

    plane = [device(*ahead(i, j), y, c) for i, j in shifts]
    greet([to_yp, to_ym, other] + plane)
    for slot, row in enumerate((y2, yp, ym, y)):
        mail.send(slot, a_ref.at[:, :, 2 * row + (1 - c)], near.at[slot], other)
    for k, (i, j) in enumerate(shifts):
        tx, tz = ahead(i, j)
        mail.send(8 + k, m_ref.at[:, tx, tz], m_got.at[k], plane[k])

    def add_near(slot, row, part=None):
        def body(i, carry):
            near[slot, i] = (
                near[slot, i].astype(F32) + a_ref[i, :, 2 * row + c].astype(F32)
            ).astype(BF)
            return carry

        lax.fori_loop(0, 4, body, 0)

    first, second = pl.ds(0, 2), pl.ds(2, 2)
    mail.take(0, near.at[0], other)
    add_near(0, y2)
    mail.send(4, near.at[0, first], far_a, to_yp)
    mail.send(5, near.at[0, second], far_b, to_ym)
    mail.take(1, near.at[1], other)
    add_near(1, yp)
    mail.take(2, near.at[2], other)
    add_near(2, ym)
    mail.take(4, far_a, to_ym)
    near[1, first] = (near[1, first].astype(F32) + far_a[...].astype(F32)).astype(BF)
    mail.send(6, near.at[1], got_a, to_yp)
    mail.take(5, far_b, to_yp)
    near[2, second] = (near[2, second].astype(F32) + far_b[...].astype(F32)).astype(BF)
    mail.send(7, near.at[2], got_b, to_ym)
    mail.take(3, near.at[3], other)
    add_near(3, y)
    mail.take(6, got_a, to_ym)
    mail.take(7, got_b, to_yp)
    total[...] = (near[3].astype(F32) + got_a[...].astype(F32) + got_b[...].astype(F32)).astype(BF)
    for k, (i, j) in enumerate(shifts):
        tx, tz = ahead(i, j)
        mail.send(23 + k, total.at[tx, tz], a_got.at[k], plane[k])
    mo[...] = m_ref[:, x, z].astype(F32)
    for k, (i, j) in enumerate(shifts):
        sx, sz = behind(i, j)
        mail.take(8 + k, m_got.at[k], device(sx, sz, y, c))
        mo[...] += m_got[k].astype(F32)
    ao[...] = total[x, z].astype(F32)
    for k, (i, j) in enumerate(shifts):
        sx, sz = behind(i, j)
        mail.take(23 + k, a_got.at[k], device(sx, sz, y, c))
        ao[...] += a_got[k].astype(F32)
    mail.finish()


def scatter_grads(m_grads, a_grads):
    return pl.pallas_call(
        grads_kernel,
        out_shape=(
            jax.ShapeDtypeStruct((3, 56, FS), F32),
            jax.ShapeDtypeStruct((16, 1024), F32),
        ),
        in_specs=[pl.BlockSpec(memory_space=pltpu.VMEM)] * 2,
        out_specs=[pl.BlockSpec(memory_space=pltpu.VMEM)] * 2,
        scratch_shapes=[
            pltpu.VMEM((15, 3, 56, FS), BF),
            pltpu.VMEM((4, 4, 4, 16, 1024), BF),
            pltpu.VMEM((2, 4, 16, 1024), BF),
            pltpu.VMEM((2, 4, 16, 1024), BF),
            pltpu.VMEM((4, 4, 16, 1024), BF),
            pltpu.VMEM((4, 4, 16, 1024), BF),
            pltpu.VMEM((4, 4, 16, 1024), BF),
            pltpu.VMEM((15, 16, 1024), BF),
            pltpu.SemaphoreType.DMA((38,)),
            pltpu.SemaphoreType.DMA((38,)),
        ],
        compiler_params=pltpu.CompilerParams(
            collective_id=2, has_side_effects=True, vmem_limit_bytes=48 * 1024 * 1024
        ),
        name="scatter_grads",
    )(m_grads, a_grads)


def select_matrix():
    pick = np.zeros((226, 256), np.float32)
    for k in range(16):
        for r in range(7):
            pick[7 * k + r, 16 * k + r] = 1
            pick[112 + 7 * k + r, 16 * k + 8 + r] = 1
        pick[224, 16 * k + 7] = 1
        pick[225, 16 * k + 15] = 1
    return pick


def pack_attention(gain_one, w_qkv, b_qkv, w_out, gain_two):
    index = lax.axis_index("dp") * 8 + lax.axis_index("ctx")
    within = lax.rem(index, 16)
    zeros = jnp.zeros((LAYERS, D), BF)
    one = lax.dynamic_update_slice(zeros, gain_one, (0, 7 * index))
    two = lax.dynamic_update_slice(zeros, gain_two, (0, 7 * index))
    bias = lax.dynamic_update_slice(jnp.zeros((LAYERS, 256), BF), b_qkv, (0, 9 * within))
    row_seven = jnp.concatenate([one, bias[:, :128]], axis=1)[:, None]
    row_last = jnp.concatenate([two, bias[:, 128:]], axis=1)[:, None]
    joined = jnp.concatenate([w_qkv, w_out], axis=2)
    return jnp.concatenate([joined[:, :, :1024], row_seven, joined[:, :, 1024:], row_last], axis=1)


def unpack_attention(block, pick):
    groups = block.reshape(8, 256, 1024)
    out = jnp.einsum("ab,gbc->gac", pick, groups, preferred_element_type=F32).astype(BF)
    low = out[:, :112].reshape(D, 1024)
    high = out[:, 112:224].reshape(D, 1024)
    spare = out[:, 224:]
    gain_one = jnp.sum(spare[:, 0, :D].astype(F32), axis=0)
    gain_two = jnp.sum(spare[:, 1, :D].astype(F32), axis=0)
    bias = jnp.concatenate([spare[:, 0, D:], spare[:, 1, D : D + 16]], axis=1).reshape(QKV)
    qkv = jnp.concatenate([low, high[:, :128]], axis=1)
    return gain_one, qkv, bias, high[:, 128:], gain_two


def pack_attention_grads(gain_one, qkv, qk_bias, value_bias, out, gain_two, pick):
    low = qkv[:, :1024].astype(BF).reshape(8, 112, 1024)
    high = jnp.concatenate([qkv[:, 1024:], out], axis=1).astype(BF).reshape(8, 112, 1024)
    row_seven = jnp.concatenate(
        [jnp.broadcast_to(gain_one[None], (8, D)), qk_bias.reshape(8, 128)], axis=1
    )
    row_last = jnp.concatenate(
        [
            jnp.broadcast_to(gain_two[None], (8, D)),
            value_bias.reshape(8, 16),
            jnp.zeros((8, 112), F32),
        ],
        axis=1,
    )
    rows = jnp.concatenate(
        [low, high, row_seven.astype(BF)[:, None], row_last.astype(BF)[:, None]], axis=1
    )
    block = jnp.einsum("ab,gac->gbc", pick, rows, preferred_element_type=F32).astype(BF)
    return block.reshape(4, 4, 8, 16, 1024)


def unpack_attention_grads(block):
    index = lax.axis_index("dp") * 8 + lax.axis_index("ctx")
    within = lax.rem(index, 16)
    qkv = jnp.concatenate([block[:7], block[8:15, :128]], axis=1)
    out = block[8:15, 128:]
    gain_one = lax.dynamic_slice(block[7], (7 * index,), (7,))
    gain_two = lax.dynamic_slice(block[15], (7 * index,), (7,))
    qk_bias = lax.dynamic_slice(block[7], (D + 8 * within,), (8,))
    value_bias = lax.dynamic_slice(block[15], (D + within,), (1,))
    return gain_one, qkv, qk_bias, value_bias, out, gain_two


def norm_scale(inputs, gain_vec):
    return (
        inputs * lax.rsqrt(jnp.mean(inputs * inputs, axis=-1, keepdims=True) + eps_norm) * gain_vec
    )


def rotate(inputs, tables):
    cosine_table, sine_table = tables
    half_dim = inputs.shape[-1] // 2
    lower_half = inputs[..., :half_dim]
    upper_half = inputs[..., half_dim:]
    return jnp.concatenate(
        [
            lower_half * cosine_table - upper_half * sine_table,
            upper_half * cosine_table + lower_half * sine_table,
        ],
        axis=-1,
    )


def rotate_back(inputs, tables):
    return rotate(inputs, (tables[0], -tables[1]))


def swiglu(gate_pre, up_pre):
    return jax.nn.silu(gate_pre) * up_pre


def inner_rows(left_side, right_side):
    return lax.dot_general(
        left_side, right_side, (((0,), (0,)), ((), ())), preferred_element_type=F32
    )


def times_transposed(left_side, right_side):
    return lax.dot_general(
        left_side, right_side, (((1,), (1,)), ((), ())), preferred_element_type=F32
    )


def masked_scores(queries, keys_all, allowed):
    scores = jnp.einsum(
        "skgd,tkd->kgst", queries, keys_all, preferred_element_type=F32
    ) * queries.shape[-1] ** (-0.5)
    return jnp.where(allowed[None, None], scores, neg_fill)


def attend(queries, keys_all, values_all, allowed):
    scores = masked_scores(queries, keys_all, allowed)
    highest = jnp.max(scores, axis=-1, keepdims=True)
    log_total = highest + jnp.log(jnp.sum(jnp.exp(scores - highest), axis=-1, keepdims=True))
    soft_weights = jnp.exp(scores - log_total).astype(BF)
    output = jnp.einsum("kgst,tkd->skgd", soft_weights, values_all, preferred_element_type=F32)
    return (output, log_total)


def attend_back(queries, keys_all, values_all, log_total, grad_out, allowed):
    scale = queries.shape[-1] ** (-0.5)
    soft_weights = jnp.exp(masked_scores(queries, keys_all, allowed) - log_total)
    grad_soft = jnp.einsum("skgd,tkd->kgst", grad_out, values_all, preferred_element_type=F32)
    grad_values = jnp.einsum(
        "kgst,skgd->tkd", soft_weights.astype(BF), grad_out, preferred_element_type=F32
    )
    grad_scores = soft_weights * (
        grad_soft - jnp.sum(grad_soft * soft_weights, axis=-1, keepdims=True)
    )
    grad_scores = grad_scores.astype(BF)
    grad_queries = (
        jnp.einsum("kgst,tkd->skgd", grad_scores, keys_all, preferred_element_type=F32) * scale
    )
    grad_keys = (
        jnp.einsum("kgst,skgd->tkd", grad_scores, queries, preferred_element_type=F32) * scale
    )
    return (grad_queries, grad_keys, grad_values)


def layer_forward(inputs, weights, tables, allowed):
    gain_first, qkv_weight, qkv_bias, out_weight, gain_second, gate_weight, up_weight, down_weight = weights
    kv_width = KVH * HD
    groups = H // KVH
    tokens_here = inputs.shape[0]
    hidden = norm_scale(inputs, gain_first).astype(BF)
    packed = jnp.dot(hidden, qkv_weight, preferred_element_type=F32) + qkv_bias.astype(F32)
    queries = rotate(packed[:, :D].reshape(tokens_here, H, HD), tables).astype(BF)
    keys_here = rotate(packed[:, D : D + kv_width].reshape(tokens_here, KVH, HD), tables).astype(BF)
    values_here = packed[:, D + kv_width :].astype(BF)
    both = ctx_gather(
        jnp.concatenate([keys_here.reshape(tokens_here, kv_width), values_here], axis=1), 3
    )
    whole_len = both.shape[0]
    keys_all = both[:, :kv_width].reshape(whole_len, KVH, HD)
    values_all = both[:, kv_width:].reshape(whole_len, KVH, HD)
    queries_seq = queries.reshape(tokens_here, KVH, groups, HD)
    attended, log_total = attend(queries_seq, keys_all, values_all, allowed)
    attended = attended.reshape(tokens_here, D).astype(BF)
    after_attn = inputs + jnp.dot(attended, out_weight, preferred_element_type=F32)
    hidden_two = norm_scale(after_attn, gain_second).astype(BF)
    hidden_rows = ctx_gather(hidden_two, 4)
    gate_pre = jnp.dot(hidden_rows, gate_weight, preferred_element_type=F32)
    up_pre = jnp.dot(hidden_rows, up_weight, preferred_element_type=F32)
    activated = swiglu(gate_pre, up_pre).astype(BF)
    partial_out = times_transposed(activated, down_weight).astype(BF)
    output = after_attn + ctx_scatter(partial_out, 5)
    kept = (
        inputs,
        hidden,
        queries_seq,
        keys_all,
        values_all,
        log_total,
        attended,
        after_attn,
        hidden_rows,
        gate_pre,
        up_pre,
        activated,
    )
    return (output, kept)


def layer_backward(grad_output, kept, weights, tables, allowed, pick):
    gain_first, qkv_weight, qkv_bias, out_weight, gain_second, gate_weight, up_weight, down_weight = weights
    (
        inputs,
        hidden,
        queries_seq,
        keys_all,
        values_all,
        log_total,
        attended,
        after_attn,
        hidden_rows,
        gate_pre,
        up_pre,
        activated,
    ) = kept
    tokens_here = inputs.shape[0]
    kv_width = KVH * HD
    down_in = ctx_gather(grad_output.astype(BF), 4)
    grad_down = inner_rows(down_in, activated)
    grad_act = jnp.dot(down_in, down_weight, preferred_element_type=F32)
    unused_out, swiglu_back = jax.vjp(swiglu, gate_pre, up_pre)
    grad_gate, grad_up = swiglu_back(grad_act)
    grad_gate = grad_gate.astype(BF)
    grad_up = grad_up.astype(BF)
    grad_gate_w = inner_rows(hidden_rows, grad_gate)
    grad_up_w = inner_rows(hidden_rows, grad_up)
    partial_hidden = times_transposed(grad_gate, gate_weight) + times_transposed(grad_up, up_weight)
    grad_hidden_two = ctx_scatter(partial_hidden.astype(BF), 5)
    unused_out, norm_back_second = jax.vjp(norm_scale, after_attn, gain_second)
    grad_mid, grad_gain_second = norm_back_second(grad_hidden_two)
    grad_mid = grad_mid + grad_output
    attn_in = grad_mid.astype(BF)
    grad_out_w = inner_rows(attended, attn_in)
    grad_attended = times_transposed(attn_in, out_weight).astype(BF).reshape(queries_seq.shape)
    grad_queries, grad_keys, grad_values = attend_back(
        queries_seq, keys_all, values_all, log_total, grad_attended, allowed
    )
    whole_len = keys_all.shape[0]
    both = ctx_scatter(
        jnp.concatenate(
            [grad_keys.reshape(whole_len, kv_width), grad_values.reshape(whole_len, kv_width)],
            axis=1,
        ).astype(BF),
        6,
    )
    grad_keys = both[:, :kv_width]
    grad_values = both[:, kv_width:]
    grad_query_flat = rotate_back(grad_queries.reshape(tokens_here, H, HD), tables).reshape(
        tokens_here, D
    )
    grad_key_flat = rotate_back(grad_keys.reshape(tokens_here, KVH, HD), tables).reshape(
        tokens_here, kv_width
    )
    grad_packed = jnp.concatenate([grad_query_flat, grad_key_flat, grad_values], axis=1).astype(BF)
    grad_qkv_w = inner_rows(hidden, grad_packed)
    grad_qkv_b = jnp.sum(grad_packed.astype(F32), axis=0)
    grad_hidden = times_transposed(grad_packed, qkv_weight)
    unused_out, norm_back_first = jax.vjp(norm_scale, inputs, gain_first)
    grad_input, grad_gain_first = norm_back_first(grad_hidden)
    grad_input = grad_input + grad_mid
    a_grads = pack_attention_grads(
        grad_gain_first,
        grad_qkv_w,
        grad_qkv_b[: D + kv_width],
        grad_qkv_b[D + kv_width :],
        grad_out_w,
        grad_gain_second,
        pick,
    )
    m_grads = jnp.stack([grad_gate_w, grad_up_w, grad_down]).astype(BF).reshape(3, 4, 4, 56, FS)
    m_sum, a_sum = scatter_grads(m_grads, a_grads)
    sums = unpack_attention_grads(a_sum) + (m_sum[0], m_sum[1], m_sum[2].T)
    return (grad_input, sums)


def shards(
    tokens, cotangent, span_order, gain_one, w_qkv, b_qkv, w_out, gain_two, w_gate, w_up, w_down
):
    sequences, local_len, width = tokens.shape
    span_len = local_len // 2
    ctx_place = lax.axis_index("ctx")
    offsets = jnp.arange(span_len, dtype=jnp.int32)
    local_spans = lax.dynamic_slice_in_dim(span_order, 2 * ctx_place, 2)
    local_pos = (local_spans[:, None] * span_len + offsets[None, :]).reshape(local_len)
    all_pos = (span_order[:, None] * span_len + offsets[None, :]).reshape(-1)
    allowed = all_pos[None, :] <= local_pos[:, None]
    frequency = rope_base ** (-jnp.arange(HD // 2, dtype=F32) * 2.0 / HD)
    angles = local_pos.astype(F32)[:, None] * frequency[None, :]
    tables = (jnp.cos(angles)[:, None, :], jnp.sin(angles)[:, None, :])
    pick = jnp.asarray(select_matrix(), BF)

    m_block = jnp.stack([w_gate, w_up, w_down.transpose(0, 2, 1)], axis=1).reshape(6, 56, FS)
    a_block = pack_attention(gain_one, w_qkv, b_qkv, w_out, gain_two)
    m_full, a_full = gather_weights(m_block, a_block)
    m_full = m_full.reshape(2, 3, D, FS)
    weights = [
        unpack_attention(a_full[l], pick) + (m_full[l, 0], m_full[l, 1], m_full[l, 2])
        for l in range(LAYERS)
    ]
    state = tokens.reshape(local_len, width).astype(F32)
    kept_layers = []
    for l in range(LAYERS):
        state, kept = layer_forward(state, weights[l], tables, allowed)
        kept_layers.append(kept)
    grad_state = cotangent.reshape(local_len, width).astype(F32)
    grad_layers = []
    for l in reversed(range(LAYERS)):
        grad_state, sums = layer_backward(
            grad_state, kept_layers[l], weights[l], tables, allowed, pick
        )
        grad_layers.insert(0, sums)
    stacks = [jnp.stack([sums[member] for sums in grad_layers]) for member in range(9)]
    output = state.astype(BF).reshape(sequences, local_len, width)
    input_grad = grad_state.reshape(sequences, local_len, width)
    return (output, input_grad) + tuple(stacks)


def solution(mesh):
    return jax.shard_map(
        shards,
        mesh=mesh,
        in_specs=(
            P("dp", "ctx", None),
            P("dp", "ctx", None),
            P(),
            P(None, ("dp", "ctx")),
            P(None, ("dp", "ctx"), None),
            P(None, ("dp", "ctx")),
            P(None, ("dp", "ctx"), None),
            P(None, ("dp", "ctx")),
            P(None, "dp", "ctx"),
            P(None, "dp", "ctx"),
            P(None, "ctx", "dp"),
        ),
        out_specs=(
            P("dp", "ctx", None),
            P("dp", "ctx", None),
            P(None, ("dp", "ctx")),
            P(None, ("dp", "ctx"), None),
            P(None, ("dp", "ctx")),
            P(None, ("dp", "ctx")),
            P(None, ("dp", "ctx"), None),
            P(None, ("dp", "ctx")),
            P(None, "dp", "ctx"),
            P(None, "dp", "ctx"),
            P(None, "ctx", "dp"),
        ),
        check_vma=False,
    )
```

time: 1640 us -> 603 us (0.37)
  waiting for transfers between devices: 1220 us -> 0 us
  Pallas kernels: 0 us -> 355 us
  blocking collectives: 184 us -> 0 us
  local copies, waits for them, and re-layouts: 33.6 us -> 79.6 us
  matrix products: 141 us -> 124 us
    unnamed x40 -> x0, waiting for transfers between devices: 633 us -> none
    all_gather x14 -> x0, waiting for transfers between devices: 464 us -> none  [the longest x2 79.4 us: fetch_forward(): lax.all_gather(current[5], 'dp', axis=0, tiled=True)]
    pallas_call x0 -> x15, Pallas kernels: none -> 355 us  [the longest x2 130 us: scatter_grads(): pl.pallas_call(grads_kernel, out_shape=(jax.ShapeDtypeStruct((3, 56, FS),...]
    unnamed x2 -> x0, blocking collectives: 135 us -> none
    reduce_scatter x4 -> x0, waiting for transfers between devices: 124 us -> none  [the longest x2 62.3 us: layer_forward(): lax.psum_scatter(partial_out.astype(jnp.bfloat16), 'ctx', scatter_dimensi...]
    all_gather x4 -> x0, blocking collectives: 48.9 us -> none  [the longest x2 25.9 us: layer_forward(): lax.all_gather(values_here.reshape(sequences, local_len, kv_width), 'ctx'...]
    concatenate x0 -> x20, local copies, waits for them, and re-layouts: none -> 18.8 us  [the longest x8 14.6 us: layer_backward(): jnp.concatenate([grad_keys.reshape(whole_len, kv_width), grad_values.resh...]
    slice x19 -> x47, local copies, waits for them, and re-layouts: 7.19 us -> 24 us  [the longest x2 4.54 us: unpack_attention(): low = out[:, :112].reshape(D, 1024)]
  transfers between devices with their start and end apart: 29 -> 0, of which waited for: 27 -> 0; matrix products, arithmetic and copies ran while one was open for 8% -> 0% of each run, Pallas kernels for 0% -> 0%
where the time goes in v1:
time: 603 us; the launch traced here: 598 us
  Pallas kernels  355 us (59%)
  matrix products  124 us (21%)
  local copies, waits for them, and re-layouts  79.6 us (13%)
  other arithmetic  36.3 us (6%)
    pallas_call x2, Pallas kernels, scatter_grads(): pl.pallas_call(grads_kernel, out_shape=(jax.ShapeDtypeStruct((3, 56, FS),...  130 us
    pallas_call x6, Pallas kernels, ctx_gather(): pl.pallas_call(functools.partial(ctx_gather_kernel, rows), out_shape=jax....  82 us
    pallas_call x6, Pallas kernels, ctx_scatter(): pl.pallas_call(functools.partial(ctx_scatter_kernel, rows), out_shape=jax...  78.2 us
    pallas_call x1, Pallas kernels, gather_weights(): pl.pallas_call(weights_kernel, out_shape=(jax.ShapeDtypeStruct((6, 4, 4,...  65.5 us
    dot_general x10, matrix products, inner_rows(): lax.dot_general(left_side, right_side, (((0,), (0,)), ((), ())), preferre...  24 us
    dot_general x10, matrix products, times_transposed(): lax.dot_general(left_side, right_side, (((1,), (1,)), ((), ())), preferre...  23.2 us
    concatenate x8, local copies, waits for them, and re-layouts, layer_backward(): jnp.concatenate([grad_keys.reshape(whole_len, kv_width), grad_values.resh...  14.6 us
    dot_general x4, local copies, waits for them, and re-layouts, inner_rows(): lax.dot_general(left_side, right_side, (((0,), (0,)), ((), ())), preferre...  13.8 us

profile of v1, /device:TPU:0, one launch (start us, length us, event | category | flops | bytes accessed | tf_op | source)
XLA Modules:
  0.0 598.4 jit_solution(10475993542635261064)
XLA Ops:
  11.9 15.7 %ctx_gather_896.6 = bf16[4,2,128,896]{3,2,1,0:T(8,128)(2,1)} custom-call(bf16[128,896]{1,0:T(8,128)(2,1)} %bitcast.458), custom_call_target="tpu_custom_call" | custom-call | tf_op jit(solution)/shard_map/ctx_gather_896/pallas_call | solution.py:238
  27.6 65.5 %gather_weights.1 = (bf16[6,4,4,56,608]{4,3,2,1,0:T(8,128)(2,1)}, bf16[2,4,4,8,16,1024]{5,4,3,2,1,0:T(8,128)(2,1)}) custom-call(bf16[6,56,608]{2,1,0:T(8,128)(2,1)} %bitcast.437, bf16[2,16,1024]{2,1,0:T(8,128)(2,1)} %fusion.129.a_ref), custom_call_target="tpu_custom_call" | custom-call | tf_op jit(solution)/shard_map/gather_weights/pallas_call | solution.py:186
  93.1 4.2 fusion.167
  97.3 3.7 convert_bitcast_fusion
  101.0 1.9 convert_bitcast_fusion.1
  102.9 1.8 copy-done.12
  108.0 2.8 fusion.169
  117.9 9.6 %ctx_gather_256.2 = bf16[4,2,128,256]{3,2,1,0:T(8,128)(2,1)} custom-call(bf16[128,256]{1,0:T(8,128)(2,1)} %pad_maximum_fusion.26.v_ref), custom_call_target="tpu_custom_call" | custom-call | tf_op jit(solution)/shard_map/ctx_gather_256/pallas_call | solution.py:238
  133.1 1.8 convolution_convert_fusion.13
  136.3 16.1 %ctx_gather_896.4 = bf16[4,2,128,896]{3,2,1,0:T(8,128)(2,1)} custom-call(bf16[128,896]{1,0:T(8,128)(2,1)} %multiply_convert_fusion.5.v_ref), custom_call_target="tpu_custom_call" | custom-call | tf_op jit(solution)/shard_map/ctx_gather_896/pallas_call | solution.py:238
  152.4 4.2 copy.143
  156.7 2.8 fusion.101
  159.4 5.4 multiply_convert_fusion.2
  164.8 3.5 convolution_convert_fusion.3
  168.4 14.6 %ctx_scatter_896.4 = f32[128,896]{1,0:T(8,128)S(1)} custom-call(bf16[4,2,128,896]{3,2,1,0:T(8,128)(2,1)S(1)} %bitcast.384), custom_call_target="tpu_custom_call" | custom-call | tf_op jit(solution)/shard_map/ctx_scatter_896/pallas_call | solution.py:293
  185.1 11.1 %ctx_gather_256.3 = bf16[4,2,128,256]{3,2,1,0:T(8,128)(2,1)} custom-call(bf16[128,256]{1,0:T(8,128)(2,1)} %pad_maximum_fusion.27.v_ref), custom_call_target="tpu_custom_call" | custom-call | tf_op jit(solution)/shard_map/ctx_gather_256/pallas_call | solution.py:238
  205.7 14.7 %ctx_gather_896.5 = bf16[4,2,128,896]{3,2,1,0:T(8,128)(2,1)} custom-call(bf16[128,896]{1,0:T(8,128)(2,1)} %multiply_convert_fusion.3.v_ref), custom_call_target="tpu_custom_call" | custom-call | tf_op jit(solution)/shard_map/ctx_gather_896/pallas_call | solution.py:238
  220.4 4.3 copy.147
  224.7 2.8 fusion.106
  227.5 2.9 fusion.105
  230.4 5.2 fusion.48
  238.5 3.1 fusion.69
  244.7 1.8 convolution_convert_fusion.2
  246.5 15.6 %ctx_scatter_896.5 = f32[128,896]{1,0:T(8,128)S(1)} custom-call(bf16[4,2,128,896]{3,2,1,0:T(8,128)(2,1)S(1)} %bitcast.383), custom_call_target="tpu_custom_call" | custom-call | tf_op jit(solution)/shard_map/ctx_scatter_896/pallas_call | solution.py:293
  262.1 1.8 fusion.104
  263.9 1.8 add_convert_fusion.1
  265.8 15.0 %ctx_scatter_896.6 = f32[128,896]{1,0:T(8,128)S(1)} custom-call(bf16[4,2,128,896]{3,2,1,0:T(8,128)(2,1)S(1)} %bitcast.382), custom_call_target="tpu_custom_call" | custom-call | tf_op jit(solution)/shard_map/ctx_scatter_896/pallas_call | solution.py:293
  284.9 5.6 fusion.99
  290.5 1.8 concatenate.202
  292.3 1.8 copy.132
  295.0 3.0 convolution_convert_fusion.4
  298.0 5.6 fusion.3
  303.7 2.2 fusion.5
  305.9 1.9 fusion.97
  309.4 1.8 concatenate.201
  311.2 1.8 copy.131
  314.1 8.8 %ctx_scatter_256.2 = f32[128,256]{1,0:T(8,128)S(1)} custom-call(bf16[4,2,128,256]{3,2,1,0:T(8,128)(2,1)S(1)} %pad_maximum_fusion.8.p_ref), custom_call_target="tpu_custom_call" | custom-call | tf_op jit(solution)/shard_map/ctx_scatter_256/pallas_call | solution.py:293
  326.2 2.7 multiply_reduce_fusion.1
  333.9 14.9 %ctx_gather_896.7 = bf16[4,2,128,896]{3,2,1,0:T(8,128)(2,1)} custom-call(bf16[128,896]{1,0:T(8,128)(2,1)} %get-tuple-element.68.v_ref), custom_call_target="tpu_custom_call" | custom-call | tf_op jit(solution)/shard_map/ctx_gather_896/pallas_call | solution.py:238
  348.8 5.8 multiply_convert_fusion
  354.7 2.7 fusion.66
  357.3 2.7 fusion.65
  360.0 3.8 copy.144
  363.8 3.6 fusion.67
  367.5 2.4 pad_maximum_fusion.m_ref
  369.9 3.2 fusion.100
  373.1 3.2 add_convert_fusion
  376.3 15.0 %ctx_scatter_896.7 = f32[128,896]{1,0:T(8,128)S(1)} custom-call(bf16[4,2,128,896]{3,2,1,0:T(8,128)(2,1)S(1)} %bitcast.381), custom_call_target="tpu_custom_call" | custom-call | tf_op jit(solution)/shard_map/ctx_scatter_896/pallas_call | solution.py:293
  396.8 5.6 fusion.98
  402.3 1.8 concatenate.208
  404.2 1.8 copy.140
  406.8 3.1 convolution_convert_fusion.5
  409.9 5.6 fusion
  415.6 2.2 fusion.2
  417.8 1.9 fusion.96
  421.3 1.8 concatenate.207
  423.1 1.8 copy.139
  426.0 9.3 %ctx_scatter_256.3 = f32[128,256]{1,0:T(8,128)S(1)} custom-call(bf16[4,2,128,256]{3,2,1,0:T(8,128)(2,1)S(1)} %pad_maximum_fusion.9.p_ref), custom_call_target="tpu_custom_call" | custom-call | tf_op jit(solution)/shard_map/ctx_scatter_256/pallas_call | solution.py:293
  440.6 2.6 fusion.111
  446.2 6.1 %fusion.36 = bf16[8,1024,256]{1,2,0:T(8,128)(2,1)} fusion(bf16[226,256,1]{1,0,2:T(8,128)(2,1)} %constant.102, bf16[8,1,16]{2,1,0:T(2,128)(2,1)S(1)} %concatenate.230, bf16[8,1,128]{2,1,0:T(2,128)(2,1)S(1)} %copy.149, bf16[8,112,896]{2,1,0:T(8,128)(2,1)} %convolution_convert_fusion.4, bf16[8,112,128]{2,1,0:T(8,128)(2,1)} %bitcast.469, ...), kind=kOutput, calls=%fused_computation.56 | convolution fusion | flops 979632128 | bytes 9370880 | tf_op jit(solution)/shard_map/ab,gac->gbc/dot_general | solution.py:464
  452.4 66.6 %scatter_grads.3 = (f32[3,56,608]{2,1,0:T(8,128)S(1)}, f32[16,1024]{1,0:T(8,128)S(1)}) custom-call(bf16[3,4,4,56,608]{4,3,2,1,0:T(8,128)(2,1)S(1)} %pad_maximum_fusion.1.m_ref, bf16[4,4,8,16,1024]{4,3,2,1,0:T(8,128)(2,1)} %bitcast.407), custom_call_target="tpu_custom_call" | custom-call | tf_op jit(solution)/shard_map/scatter_grads/pallas_call | solution.py:383
  520.1 2.0 convolution_convert_fusion.1
  522.5 4.6 fusion.39
  527.1 63.1 %scatter_grads.2 = (f32[3,56,608]{2,1,0:T(8,128)S(1)}, f32[16,1024]{1,0:T(8,128)S(1)}) custom-call(bf16[3,4,4,56,608]{4,3,2,1,0:T(8,128)(2,1)S(1)} %copy-done, bf16[4,4,8,16,1024]{4,3,2,1,0:T(8,128)(2,1)} %bitcast.406), custom_call_target="tpu_custom_call" | custom-call | tf_op jit(solution)/shard_map/scatter_grads/pallas_call | solution.py:383
  (381 shorter events, 87.8 us)
Async XLA Ops:
  3.0 113.0 %copy-start.74 = (f32[128]{0:T(128)}, f32[128]{0:T(128)S(1)}, u32[]{:S(2)}) copy-start(f32[128]{0:T(128)S(1)} %fusion.141) | copy-start | bytes 1540
  9.0 191.3 %copy-start.3 = (pred[128,1024]{0,1:T(8,128)(4,1)}, pred[128,1024]{0,1:T(8,128)(4,1)S(1)}, u32[]{:S(2)}) copy-start(pred[128,1024]{0,1:T(8,128)(4,1)S(1)} %broadcast_compare_fusion) | copy-start | bytes 393220
  93.1 4.2 copy-start.57
  108.0 3.2 copy-start.11
  110.8 5.2 copy-start.35
  110.8 24.1 %copy-start.6 = (bf16[8,112,1024]{2,1,0:T(8,128)(2,1)}, bf16[8,112,1024]{2,1,0:T(8,128)(2,1)S(1)}, u32[]{:S(2)}) copy-start(bf16[8,112,1024]{2,1,0:T(8,128)(2,1)S(1)} %get-tuple-element.82) | copy-start | bytes 5505028
  112.2 3.8 copy-start.26
  117.0 13.2 %copy-start.46 = (bf16[128,14,32]{0,2,1:T(8,128)(2,1)}, bf16[128,14,32]{0,2,1:T(8,128)(2,1)S(1)}, u32[]{:S(2)}) copy-start(bf16[128,14,32]{0,2,1:T(8,128)(2,1)S(1)} %get-tuple-element.93) | copy-start | bytes 344068
  117.0 13.2 %copy-start.48 = (bf16[128,14,32]{0,2,1:T(8,128)(2,1)}, bf16[128,14,32]{0,2,1:T(8,128)(2,1)S(1)}, u32[]{:S(2)}) copy-start(bf16[128,14,32]{0,2,1:T(8,128)(2,1)S(1)} %get-tuple-element.94) | copy-start | bytes 344068
  130.2 2.9 copy-start.1
  134.9 21.7 %copy-start.55 = (bf16[2,64,7,128]{3,1,2,0:T(8,128)(2,1)}, bf16[2,64,7,128]{3,1,2,0:T(8,128)(2,1)S(1)}, u32[]{:S(2)}) copy-start(bf16[2,64,7,128]{3,1,2,0:T(8,128)(2,1)S(1)} %convolution_convert_fusion.13) | copy-start | bytes 688132
  135.5 21.2 %copy-start.80 = (f32[128]{0:T(128)}, f32[128]{0:T(128)S(1)}, u32[]{:S(2)}) copy-start(f32[128]{0:T(128)S(1)} %get-tuple-element.122) | copy-start | bytes 1540
  135.5 47.5 %copy-start.13 = (f32[128,896]{1,0:T(8,128)}, f32[128,896]{1,0:T(8,128)S(1)}, u32[]{:S(2)}) copy-start(f32[128,896]{1,0:T(8,128)S(1)} %get-tuple-element.123) | copy-start | bytes 1376260
  135.5 21.1 %copy-start.69 = (f32[128]{0:T(128)}, f32[128]{0:T(128)S(1)}, u32[]{:S(2)}) copy-start(f32[128]{0:T(128)S(1)} %fusion.142) | copy-start | bytes 1540
  152.4 4.2 copy-start.15
  159.4 5.4 copy-start.88
  164.8 3.5 copy-start.89
  168.4 14.8 %copy-start.36 = (bf16[8,112,1024]{2,1,0:T(8,128)(2,1)S(1)}, bf16[8,112,1024]{2,1,0:T(8,128)(2,1)}, u32[]{:S(2)}) copy-start(bf16[8,112,1024]{2,1,0:T(8,128)(2,1)} %get-tuple-element.79) | copy-start | bytes 5505028
  168.4 14.8 %copy-start.65 = (bf16[896,128]{1,0:T(8,128)(2,1)S(1)}, bf16[896,128]{1,0:T(8,128)(2,1)}, u32[]{:S(2)}) copy-start(bf16[896,128]{1,0:T(8,128)(2,1)} %slice.412) | copy-start | bytes 688132
  168.4 14.8 %copy-start.66 = (f32[896]{0:T(1024)S(1)}, f32[896]{0:T(1024)}, u32[]{:S(2)}) copy-start(f32[896]{0:T(1024)} %get-tuple-element.57) | copy-start | bytes 10756
  168.4 14.8 %copy-start.68 = (f32[1152]{0:T(1024)S(1)}, f32[1152]{0:T(1024)}, u32[]{:S(2)}) copy-start(f32[1152]{0:T(1024)} %reshape.764) | copy-start | bytes 13828
  183.2 20.4 %copy-start.17 = (f32[128,896]{1,0:T(8,128)}, f32[128,896]{1,0:T(8,128)S(1)}, u32[]{:S(2)}) copy-start(f32[128,896]{1,0:T(8,128)S(1)} %get-tuple-element.71) | copy-start | bytes 1376260
  184.2 14.6 %copy-start.50 = (bf16[128,14,32]{0,2,1:T(8,128)(2,1)}, bf16[128,14,32]{0,2,1:T(8,128)(2,1)S(1)}, u32[]{:S(2)}) copy-start(bf16[128,14,32]{0,2,1:T(8,128)(2,1)S(1)} %get-tuple-element.91) | copy-start | bytes 344068
  184.2 14.6 %copy-start.52 = (bf16[128,14,32]{0,2,1:T(8,128)(2,1)}, bf16[128,14,32]{0,2,1:T(8,128)(2,1)S(1)}, u32[]{:S(2)}) copy-start(bf16[128,14,32]{0,2,1:T(8,128)(2,1)S(1)} %get-tuple-element.92) | copy-start | bytes 344068
  198.8 3.0 copy-start.2
  220.4 4.3 copy-start.16
  227.5 2.9 copy-start.40
  235.6 2.9 copy-start.38
  238.5 3.1 copy-start.85
  238.5 5.6 slice-start.4
  263.9 16.9 %copy-start.24 = (f32[128,896]{1,0:T(8,128)S(1)}, f32[128,896]{1,0:T(8,128)}, u32[]{:S(2)}) copy-start(f32[128,896]{1,0:T(8,128)} %copy-done.23) | copy-start | bytes 1376260
  265.8 15.2 %copy-start.56 = (bf16[1,128,896]{2,1,0:T(8,128)(2,1)S(1)}, bf16[1,128,896]{2,1,0:T(8,128)(2,1)}, u32[]{:S(2)}) copy-start(bf16[1,128,896]{2,1,0:T(8,128)(2,1)} %param.13) | copy-start | bytes 688132
  265.8 16.0 %copy-start.10 = (bf16[8,112,1024]{2,1,0:T(8,128)(2,1)S(1)}, bf16[8,112,1024]{2,1,0:T(8,128)(2,1)}, u32[]{:S(2)}) copy-start(bf16[8,112,1024]{2,1,0:T(8,128)(2,1)} %copy-done.8) | copy-start | bytes 5505028
  295.0 8.6 %slice-start.2 = ((s8[7340032]{0:T(1024)(128)(4,1)}), s8[4194304]{0:T(1024)(128)(4,1)S(1)}, s32[]{:S(2)}) async-start(s8[7340032]{0:T(1024)(128)(4,1)} %bitcast.387), calls=%async_computation.2 | async-start | bytes 8388608
  298.0 5.6 slice-start.3
  298.0 5.6 copy-start.4
  325.3 3.7 copy-start.77
  325.3 3.7 copy-start.18
  325.3 3.7 copy-start.22
  325.3 3.7 copy-start.67
  325.3 3.7 copy-start.73
  326.2 4.7 copy-start.32
  348.8 5.8 copy-start.37
  363.8 3.6 copy-start.42
  363.8 3.6 copy-start.43
  369.9 3.2 copy-start.84
  373.1 18.2 %copy-start.14 = (f32[128,896]{1,0:T(8,128)S(1)}, f32[128,896]{1,0:T(8,128)}, u32[]{:S(2)}) copy-start(f32[128,896]{1,0:T(8,128)} %copy-done.13) | copy-start | bytes 1376260
  373.1 18.2 %copy-start.70 = (f32[128]{0:T(128)S(1)}, f32[128]{0:T(128)}, u32[]{:S(2)}) copy-start(f32[128]{0:T(128)} %copy-done.69) | copy-start | bytes 1540
  376.3 15.8 %copy-start.81 = (f32[128]{0:T(128)S(1)}, f32[128]{0:T(128)}, u32[]{:S(2)}) copy-start(f32[128]{0:T(128)} %copy-done.80) | copy-start | bytes 1540
  376.3 15.8 %copy-start.39 = (f32[128,896]{1,0:T(8,128)S(1)}, f32[128,896]{1,0:T(8,128)}, u32[]{:S(2)}) copy-start(f32[128,896]{1,0:T(8,128)} %get-tuple-element.69) | copy-start | bytes 1376260
  376.3 16.7 %copy-start.7 = (bf16[8,112,1024]{2,1,0:T(8,128)(2,1)S(1)}, bf16[8,112,1024]{2,1,0:T(8,128)(2,1)}, u32[]{:S(2)}) copy-start(bf16[8,112,1024]{2,1,0:T(8,128)(2,1)} %copy-done.6) | copy-start | bytes 5505028
  406.8 8.7 %slice-start = ((s8[7340032]{0:T(1024)(128)(4,1)}), s8[4194304]{0:T(1024)(128)(4,1)S(1)}, s32[]{:S(2)}) async-start(s8[7340032]{0:T(1024)(128)(4,1)} %bitcast.385), calls=%async_computation | async-start | bytes 8388608
  409.9 5.6 slice-start.1
  409.9 5.6 copy-start.5
  420.5 20.1 %copy-start.75 = (f32[128]{0:T(128)S(1)}, f32[128]{0:T(128)}, u32[]{:S(2)}) copy-start(f32[128]{0:T(128)} %copy-done.74) | copy-start | bytes 1540
  439.6 3.5 copy-start.33
  439.6 3.5 copy-start.34
  439.6 3.5 copy-start.61
  439.6 4.4 copy-start.20
  439.6 4.4 copy-start.27
  440.5 4.5 copy-start.63
  452.4 66.7 %copy-start.79 = (bf16[128]{0:T(256)(128)(2,1)S(1)}, bf16[128]{0:T(256)(128)(2,1)}, u32[]{:S(2)}) copy-start(bf16[128]{0:T(256)(128)(2,1)} %slice.442) | copy-start | bytes 772
  452.4 67.6 %copy-start.62 = (bf16[128,128]{0,1:T(8,128)(2,1)S(1)}, bf16[128,128]{0,1:T(8,128)(2,1)}, u32[]{:S(2)}) copy-start(bf16[128,128]{0,1:T(8,128)(2,1)} %copy.142) | copy-start | bytes 98308
  522.4 4.6 copy-start
  (34 other events, 62.8 us)
